TPU v7x, 512 devices: a whole 4x4x16 slice. The times are simulated.
512 devices in a mesh: ctx: 16 (over z), dp: 4 (over y_hi, core), tp: 8 (over y_lo, x).
Axes of the slice: x: 4, y: 4 (y_hi: 2, y_lo: 2; y = y_hi * 2 + y_lo), z: 16, core: 2. Of those that a mesh axis runs over, the one named last changes fastest.
Arguments:
- queries: bfloat16 [4, 16, 320, 3072], P('dp', 'ctx', None, 'tp'), may hold values from -8 to 8
- keys: bfloat16 [4, 16, 320, 3072], P('dp', 'ctx', None, 'tp'), may hold values from -8 to 8
- values: bfloat16 [4, 16, 320, 3072], P('dp', 'ctx', None, 'tp'), may hold values from -6 to 6
- out_grad: bfloat16 [4, 16, 320, 2560], P('dp', 'ctx', None, 'tp'), may hold values from -6 to 6
- out_weight: bfloat16 [2560, 3072], P('dp', 'tp'), may hold values from -0.109375 to 0.109375
- short_docs: int32 [4, 16, 256], P('dp', 'ctx'), may hold values from 0 to 7, never falling along the last dimension, each value on 1 to 128 neighbouring positions
- long_docs: int32 [4, 1024], P('dp'), may hold values from 0 to 1, never falling along the last dimension, each value on 1 to 768 neighbouring positions
- block_place: int32 [4, 16], P('dp'), may hold values from 0 to 15, each once within a row
Outputs:
- query_grad: bfloat16 [4, 16, 320, 3072], P('dp', 'ctx', None, 'tp')
- key_grad: bfloat16 [4, 16, 320, 3072], P('dp', 'ctx', None, 'tp')
- value_grad: bfloat16 [4, 16, 320, 3072], P('dp', 'ctx', None, 'tp')
- weight_grad: float32 [2560, 3072], P(('ctx', 'dp'), 'tp')
Inputs may be any that keep to these rules, and one draw needn't show every extreme that they name: `short_docs`: never falling along the 256 tokens, each document 1 to 128 tokens. `long_docs`: never falling along the 1024 positions, each document 1 to 768 positions. `block_place`: each row a permutation.
All inputs are finite; a program needn't handle non-finite values.
Results may differ from a plain program's by a relative error of at most 0.025.
Values may be sent and summed in bfloat16 or wider, within the bound.
A program may use at most 64 MiB of HBM per device.

v0:
```python
import jax
import jax.numpy as jnp
from jax import lax
from jax.sharding import PartitionSpec as P

HD = 128
LOC = 256


NEG = -1e30


def split_heads(block, count):
    return block.reshape(block.shape[0], count, block.shape[1] // count)


def block_positions(length, place, block):
    rows = jnp.arange(length, dtype=jnp.int32)
    owner = rows // block
    table = jnp.arange(place.shape[0], dtype=jnp.int32)
    picked = jnp.sum(jnp.where(owner[:, None] == table[None, :], place[None, :], 0), axis=1)
    return picked * block + rows % block


def local_attend(qh, kh, vh, gh, mask, scale):
    scores = jnp.einsum("qhd,khd->hqk", qh, kh, preferred_element_type=jnp.float32) * scale
    scores = jnp.where(mask[None], scores, NEG)
    top = jnp.max(scores, axis=2, keepdims=True)
    lse = top + jnp.log(jnp.sum(jnp.exp(scores - top), axis=2, keepdims=True))
    prob = jnp.where(mask[None], jnp.exp(scores - lse), 0.0)
    weights = prob.astype(jnp.bfloat16)
    attn = jnp.einsum("hqk,khd->qhd", weights, vh, preferred_element_type=jnp.float32).astype(
        jnp.bfloat16
    )
    delta = jnp.sum(gh.astype(jnp.float32) * attn.astype(jnp.float32), axis=2).T[:, :, None]
    dpv = jnp.einsum("qhd,khd->hqk", gh, vh, preferred_element_type=jnp.float32)
    dsc = (prob * (dpv - delta)).astype(jnp.bfloat16)
    dq = jnp.einsum("hqk,khd->qhd", dsc, kh, preferred_element_type=jnp.float32) * scale
    dk = jnp.einsum("hqk,qhd->khd", dsc, qh, preferred_element_type=jnp.float32) * scale
    dv = jnp.einsum("hqk,qhd->khd", weights, gh, preferred_element_type=jnp.float32)
    count = qh.shape[0]
    flat = lambda t: t.reshape(count, -1).astype(jnp.bfloat16)
    return (flat(attn), flat(dq), flat(dk), flat(dv))


def local(queries, keys, values, out_grad, out_weight, short_docs, long_docs, block_place):
    rows = queries.shape[2]
    feats = queries.shape[3]
    count = feats // HD
    block = rows - LOC
    scale = HD ** (-0.5)
    place = block_place[0]
    long_ids = long_docs[0]
    me = lax.axis_index("ctx")
    q_all = queries[0, 0]
    k_all = keys[0, 0]
    v_all = values[0, 0]
    grads_full = lax.all_gather(out_grad[0, 0], "tp", axis=1, tiled=True)
    cols = grads_full
    grad_all = jnp.dot(
        cols,
        lax.all_gather(out_weight, "dp", axis=0, tiled=True),
        preferred_element_type=jnp.float32,
    ).astype(jnp.bfloat16)
    spots = jnp.arange(LOC)
    sids = short_docs[0, 0]
    smask = (spots[None, :] <= spots[:, None]) & (sids[None, :] == sids[:, None])
    attn_s, dq_s, dk_s, dv_s = local_attend(
        split_heads(q_all[:LOC], count),
        split_heads(k_all[:LOC], count),
        split_heads(v_all[:LOC], count),
        split_heads(grad_all[:LOC], count),
        smask,
        scale,
    )
    q_long = q_all[LOC:]
    k_long = k_all[LOC:]
    v_long = v_all[LOC:]
    g_long = grad_all[LOC:]
    ql = split_heads(q_long, count)
    kl = split_heads(k_long, count)
    vl = split_heads(v_long, count)
    gl = split_heads(g_long, count)
    my_block = jnp.sum(jnp.where(jnp.arange(place.shape[0]) == me, place, 0))
    qpos = my_block * block + jnp.arange(block, dtype=jnp.int32)
    qid = jnp.take(long_ids, qpos)

    def key_mask(length):
        kpos = block_positions(length, place, block)
        kid = jnp.take(long_ids, kpos)
        return (kpos[None, :] <= qpos[:, None]) & (kid[None, :] == qid[:, None])

    piece = (
        lax.all_gather(k_long, "ctx", axis=0, tiled=True),
        lax.all_gather(v_long, "ctx", axis=0, tiled=True),
    )
    kp = split_heads(piece[0], count)
    vp = split_heads(piece[1], count)
    mask = key_mask(kp.shape[0])
    top = jnp.full((count, block, 1), NEG, jnp.float32)
    scores = jnp.einsum("qhd,khd->hqk", ql, kp, preferred_element_type=jnp.float32) * scale
    scores = jnp.where(mask[None], scores, NEG)
    new_top = jnp.maximum(top, jnp.max(scores, axis=2, keepdims=True))
    weight = jnp.where(mask[None], jnp.exp(scores - new_top), 0.0)
    total = jnp.sum(weight, axis=2, keepdims=True)
    acc = jnp.einsum(
        "hqk,khd->hqd", weight.astype(jnp.bfloat16), vp, preferred_element_type=jnp.float32
    )
    top, total, acc = (new_top, total, acc)
    lse = top + jnp.log(total)
    attn_l = (acc / total).transpose(1, 0, 2).reshape(block, feats).astype(jnp.bfloat16)
    delta_rows = jnp.sum(
        gl.astype(jnp.float32) * split_heads(attn_l, count).astype(jnp.float32), axis=2
    )
    delta = delta_rows.T[:, :, None]
    piece = (
        lax.all_gather(k_long, "ctx", axis=0, tiled=True),
        lax.all_gather(v_long, "ctx", axis=0, tiled=True),
    )
    grad_kp = split_heads(piece[0], count)
    grad_vp = split_heads(piece[1], count)
    grad_mask = key_mask(grad_kp.shape[0])
    scores = jnp.einsum("qhd,khd->hqk", ql, grad_kp, preferred_element_type=jnp.float32) * scale
    scores = jnp.where(grad_mask[None], scores, NEG)
    prob = jnp.where(grad_mask[None], jnp.exp(scores - lse), 0.0)
    dpv = jnp.einsum("qhd,khd->hqk", gl, grad_vp, preferred_element_type=jnp.float32)
    dsc = (prob * (dpv - delta)).astype(jnp.bfloat16)
    dq_acc = jnp.einsum("hqk,khd->qhd", dsc, grad_kp, preferred_element_type=jnp.float32)
    all_lse, all_delta = (
        lax.all_gather(lse[:, :, 0].T, "ctx", axis=0, tiled=True),
        lax.all_gather(delta_rows, "ctx", axis=0, tiled=True),
    )
    piece = (
        lax.all_gather(q_long, "ctx", axis=0, tiled=True),
        lax.all_gather(g_long, "ctx", axis=0, tiled=True),
    )
    qp = split_heads(piece[0], count)
    gp = split_heads(piece[1], count)
    length = qp.shape[0]
    qpos_piece = block_positions(length, place, block)
    qid_piece = jnp.take(long_ids, qpos_piece)
    mask = (qpos[None, :] <= qpos_piece[:, None]) & (qid[None, :] == qid_piece[:, None])
    lse_piece = all_lse.T[:, :, None]
    delta_piece = all_delta.T[:, :, None]
    scores = jnp.einsum("qhd,khd->hqk", qp, kl, preferred_element_type=jnp.float32) * scale
    scores = jnp.where(mask[None], scores, NEG)
    prob = jnp.where(mask[None], jnp.exp(scores - lse_piece), 0.0)
    weights = prob.astype(jnp.bfloat16)
    dpv = jnp.einsum("qhd,khd->hqk", gp, vl, preferred_element_type=jnp.float32)
    dsc = (prob * (dpv - delta_piece)).astype(jnp.bfloat16)
    dk_acc = jnp.einsum("hqk,qhd->khd", dsc, qp, preferred_element_type=jnp.float32)
    dv_acc = jnp.einsum("hqk,qhd->khd", weights, gp, preferred_element_type=jnp.float32)
    dk_acc, dv_acc = (dk_acc, dv_acc)
    dq_l = (dq_acc * scale).reshape(block, feats).astype(jnp.bfloat16)
    dk_l = (dk_acc * scale).reshape(block, feats).astype(jnp.bfloat16)
    dv_l = dv_acc.reshape(block, feats).astype(jnp.bfloat16)
    attn_all = jnp.concatenate([attn_s, attn_l], axis=0)
    cols = grads_full
    weight_grad = lax.psum_scatter(
        lax.dot_general(
            cols, attn_all, (((0,), (0,)), ((), ())), preferred_element_type=jnp.float32
        ),
        ("ctx", "dp"),
        scatter_dimension=0,
        tiled=True,
    )
    query_grad = jnp.concatenate([dq_s, dq_l], axis=0).reshape(1, 1, rows, feats)
    key_grad = jnp.concatenate([dk_s, dk_l], axis=0).reshape(1, 1, rows, feats)
    value_grad = jnp.concatenate([dv_s, dv_l], axis=0).reshape(1, 1, rows, feats)
    return (query_grad, key_grad, value_grad, weight_grad)


def solution(mesh):
    placed = (
        P("dp", "ctx", None, "tp"),
        P("dp", "ctx", None, "tp"),
        P("dp", "ctx", None, "tp"),
        P("dp", "ctx", None, "tp"),
        P("dp", "tp"),
        P("dp", "ctx", None),
        P("dp", None),
        P("dp", None),
    )
    return jax.shard_map(
        local,
        mesh=mesh,
        in_specs=placed,
        out_specs=(
            P("dp", "ctx", None, "tp"),
            P("dp", "ctx", None, "tp"),
            P("dp", "ctx", None, "tp"),
            P(("ctx", "dp"), "tp"),
        ),
        check_vma=False,
    )
```

profile of v0, /device:TPU:6, one launch (start us, length us, event | category | flops | bytes accessed | tf_op | source)
XLA Modules:
  0.0 666.8 jit_solution(14546106580144740229)
XLA Ops:
  7.3 2.2 copy.156
  9.5 0.7 all-gather.9.cloned.1.call-update
  10.3 1.3 fusion.71
  12.2 0.7 select_reduce_fusion
  13.0 0.8 slice.40
  13.9 0.7 gather_fusion
  14.7 4.5 gather_fusion.1
  19.2 0.6 reshape.361
  20.2 0.8 copy.218
  21.0 40.2 %all-gather.1 = bf16[1,1,1024,384]{3,2,1,0:T(8,128)(2,1)S(1)} all-gather(bf16[1,1,64,384]{3,2,1,0:T(8,128)(2,1)S(1)} %slice.41), channel_id=3, replica_groups=mesh['ctx'=16,'dp'=4,'tp'=8] {'ctx'}, dimensions={2}, use_global_device_ids=true | all-gather | bytes 835584 | tf_op jit(solution)/shard_map/all_gather | solution.py:117
  61.5 31.1 %all-gather.2 = bf16[1,1,1024,384]{3,2,1,0:T(8,128)(2,1)S(1)} all-gather(bf16[1,1,64,384]{3,2,1,0:T(8,128)(2,1)S(1)} %slice.44), channel_id=4, replica_groups=mesh['ctx'=16,'dp'=4,'tp'=8] {'ctx'}, dimensions={2}, use_global_device_ids=true | all-gather | bytes 835584 | tf_op jit(solution)/shard_map/all_gather | solution.py:118
  94.3 0.5 copy-done.18
  94.8 0.8 fusion.36
  95.7 8.6 %copy.157 = bf16[1,1,320,2560]{3,2,1,0:T(8,128)(2,1)} copy(bf16[1,1,320,2560]{2,1,0,3:T(2,128)(2,1)} %all-gather.11.cloned.1.call-done) | data formatting | bytes 3276800 | tf_op jit(solution)/shard_map/all_gather | solution.py:58
  104.3 2.8 all-gather.9.cloned.1.call-done
  107.1 3.0 fusion.17
  110.2 0.6 fusion.78
  110.8 0.7 slice.51
  111.5 1.1 copy.158
  112.6 2.4 multiply_reduce_fusion.1
  115.1 0.9 copy.212
  116.0 1.8 multiply_reduce_fusion
  117.8 4.5 convolution_bitcast_fusion
  122.3 0.8 copy-done.14
  123.1 0.6 reshape.369
  123.7 0.6 reshape.367
  124.4 35.4 %all-gather.3 = bf16[1,1,1024,384]{3,2,1,0:T(8,128)(2,1)S(1)} all-gather(bf16[1,1,64,384]{3,2,1,0:T(8,128)(2,1)} %copy-done.10), channel_id=5, replica_groups=mesh['ctx'=16,'dp'=4,'tp'=8] {'ctx'}, dimensions={2}, use_global_device_ids=true | all-gather | bytes 835584 | tf_op jit(solution)/shard_map/all_gather | solution.py:134
  159.8 1.2 copy.177
  161.0 0.7 fusion.70
  161.7 27.0 %all-gather.4 = f32[16,64,3]{1,2,0:T(4,128)S(1)} all-gather(f32[1,64,3]{1,2,0:T(4,128)S(1)} %fusion.70), channel_id=1, replica_groups=mesh['ctx'=16,'dp'=4,'tp'=8] {'ctx'}, dimensions={0}, use_global_device_ids=true | all-gather | bytes 13056 | tf_op jit(solution)/shard_map/all_gather | solution.py:130
  188.8 1.3 dynamic-slice
  190.7 1.2 log_add_fusion.1
  191.9 0.7 compare_and_fusion
  192.7 2.4 fusion.8
  195.1 35.0 %all_gather.32 = bf16[1024,384]{1,0:T(8,128)(2,1)} all-gather(bf16[64,384]{1,0:T(8,128)(2,1)S(1)} %copy-done.16), channel_id=1, replica_groups=mesh['ctx'=16,'dp'=4,'tp'=8] {'ctx'}, dimensions={0}, use_global_device_ids=true | all-gather | bytes 835584 | tf_op jit(solution)/shard_map/all_gather | solution.py:135
  230.1 1.4 copy.181
  231.5 1.5 fusion.28
  233.0 0.6 copy.241
  233.7 2.4 fusion.30
  236.0 0.8 copy.243
  236.9 26.3 %all-gather.5 = f32[16,64,3]{1,2,0:T(4,128)S(1)} all-gather(f32[1,64,3]{1,2,0:T(4,128)S(1)} %bitcast.150), channel_id=1, replica_groups=mesh['ctx'=16,'dp'=4,'tp'=8] {'ctx'}, dimensions={0}, use_global_device_ids=true | all-gather | bytes 13056 | tf_op jit(solution)/shard_map/all_gather | solution.py:131
  263.2 1.9 fusion.29
  267.0 0.7 maximum_bitcast_fusion.2
  267.7 0.7 maximum_bitcast_fusion
  268.4 0.7 maximum_bitcast_fusion.1
  269.1 389.3 %all-reduce.3.cloned.1.call-done = f32[2560,384]{0,1:T(8,128)} async-done(((f32[2560,384]{0,1:T(8,128)}), f32[2560,384]{0,1:T(8,128)}) %all-reduce.3.cloned.1.call-update) | async-done | bytes 3932176
  658.4 1.1 constant_dynamic-slice_fusion
  659.5 0.7 copy.194
  (93 shorter events, 4.3 us)
Async XLA Ops:
  7.2 6.7 %copy-start = (s32[1,1024]{1,0:T(1,128)S(1)}, s32[1,1024]{1,0:T(1,128)}, u32[]{:S(2)}) copy-start(s32[1,1024]{1,0:T(1,128)} %param.16) | copy-start | bytes 12292
  7.2 6.6 copy-start.8
  7.2 6.7 copy-start.9
  7.2 88.5 %all-gather.11.cloned.1.call-start = ((), (), s32[]{:S(2)}) async-start(), calls=%async_computation.1 | async-start | bytes 4423680 | tf_op jit(solution)/shard_map/all_gather | solution.py:58
  9.5 97.7 %all-gather.9.cloned.1.call-start = ((), (), s32[]{:S(2)}) async-start(), calls=%async_computation | async-start | bytes 2457600 | tf_op jit(solution)/shard_map/all_gather | solution.py:62
  10.2 648.2 %all-reduce.3.cloned.1.call-start = ((), (), s32[]{:S(2)}) async-start(), calls=%async_computation.2 | async-start | bytes 7864320
  13.8 5.4 copy-start.10
  13.8 7.2 %copy-start.11 = (bf16[1,1,64,384]{3,2,1,0:T(8,128)(2,1)}, bf16[1,1,64,384]{3,2,1,0:T(8,128)(2,1)S(1)}, u32[]{:S(2)}) copy-start(bf16[1,1,64,384]{3,2,1,0:T(8,128)(2,1)S(1)} %slice.41) | copy-start | bytes 147460
  13.9 47.6 %copy-start.13 = (bf16[1,1,64,384]{3,2,1,0:T(8,128)(2,1)}, bf16[1,1,64,384]{3,2,1,0:T(8,128)(2,1)S(1)}, u32[]{:S(2)}) copy-start(bf16[1,1,64,384]{3,2,1,0:T(8,128)(2,1)S(1)} %slice.44) | copy-start | bytes 147460
  14.6 5.2 slice-start
  14.6 5.4 slice-start.1
  14.6 5.5 slice-start.2
  20.2 72.9 %copy-start.2 = (bf16[1,1,256,384]{2,3,1,0:T(8,128)(2,1)}, bf16[1,1,256,384]{2,3,1,0:T(8,128)(2,1)S(1)}, u32[]{:S(2)}) copy-start(bf16[1,1,256,384]{2,3,1,0:T(8,128)(2,1)S(1)} %copy.216) | copy-start | bytes 589828
  61.2 31.8 %copy-start.25 = (s32[1,1,256]{2,1,0:T(1,128)S(1)}, s32[1,1,256]{2,1,0:T(1,128)}, u32[]{:S(2)}) copy-start(s32[1,1,256]{2,1,0:T(1,128)} %param.15) | copy-start | bytes 3076
  93.0 19.7 %copy-start.1 = (bf16[1,1,1024,384]{2,3,1,0:T(8,128)(2,1)}, bf16[1,1,1024,384]{2,3,1,0:T(8,128)(2,1)S(1)}, u32[]{:S(2)}) copy-start(bf16[1,1,1024,384]{2,3,1,0:T(8,128)(2,1)S(1)} %copy.168) | copy-start | bytes 2359300
  93.0 1.0 copy-start.15
  93.1 0.8 copy-start.4
  93.6 10.7 %copy-start.22 = (s32[64]{0:T(128)}, s32[64]{0:T(128)S(1)}, u32[]{:S(2)}) copy-start(s32[64]{0:T(128)S(1)} %get-tuple-element.37) | copy-start | bytes 772
  93.6 10.7 %copy-start.23 = (s32[64]{0:T(128)}, s32[64]{0:T(128)S(1)}, u32[]{:S(2)}) copy-start(s32[64]{0:T(128)S(1)} %get-tuple-element.38) | copy-start | bytes 772
  93.9 10.4 %copy-start.6 = (pred[64,1024]{1,0:T(8,128)(4,1)}, pred[64,1024]{1,0:T(8,128)(4,1)S(1)}, u32[]{:S(2)}) copy-start(pred[64,1024]{1,0:T(8,128)(4,1)S(1)} %compare_and_fusion.1) | copy-start | bytes 196612
  94.3 0.6 copy-start.18
  94.3 1.4 copy-start.21
  122.3 0.8 copy-start.14
  122.3 1.4 copy-start.12
  161.0 34.0 %copy-start.16 = (bf16[64,384]{1,0:T(8,128)(2,1)S(1)}, bf16[64,384]{1,0:T(8,128)(2,1)}, u32[]{:S(2)}) copy-start(bf16[64,384]{1,0:T(8,128)(2,1)} %get-tuple-element.25) | copy-start | bytes 147460
  195.1 38.6 %copy-start.19 = (f32[64,3]{0,1:T(4,128)S(1)}, f32[64,3]{0,1:T(4,128)}, u32[]{:S(2)}) copy-start(f32[64,3]{0,1:T(4,128)} %get-tuple-element.31) | copy-start | bytes 2308
  195.1 38.6 %copy-start.20 = (f32[3,64]{1,0:T(4,128)S(1)}, f32[3,64]{1,0:T(4,128)}, u32[]{:S(2)}) copy-start(f32[3,64]{1,0:T(4,128)} %log_add_fusion.1) | copy-start | bytes 2308
  236.0 29.2 %copy-start.5 = (pred[256,256]{0,1:T(8,128)(4,1)S(1)}, pred[256,256]{0,1:T(8,128)(4,1)}, u32[]{:S(2)}) copy-start(pred[256,256]{0,1:T(8,128)(4,1)} %copy-done.4) | copy-start | bytes 196612
  263.2 2.5 copy-start.7
  263.2 2.5 copy-start.24
  265.2 0.9 copy-start.3
  265.7 1.3 copy-start.17
Sparse Core Ops, SparseCore 0:
  10.1 60.1 all-gather.10
  72.5 34.6 all-gather.8
  122.4 535.9 all-reduce.2
where the time goes:
time: 668 us; the launch traced here: 667 us
  waiting for transfers between devices  393 us (59%)
  blocking collectives  195 us (29%)
  local copies, waits for them, and re-layouts  33.3 us (5%)
  matrix products  21.9 us (3%)
  between operations  15.6 us (2%)
  other arithmetic  8.02 us (1%)
    unnamed x4, waiting for transfers between devices  390 us
    all_gather x1, blocking collectives, local(): lax.all_gather(k_long, 'ctx', axis=0, tiled=True)  40.2 us
    all_gather x1, blocking collectives, local(): lax.all_gather(q_long, 'ctx', axis=0, tiled=True)  35.4 us
    all_gather x1, blocking collectives, local(): lax.all_gather(g_long, 'ctx', axis=0, tiled=True)  35 us
    all_gather x1, blocking collectives, local(): lax.all_gather(v_long, 'ctx', axis=0, tiled=True)  31.1 us
    all_gather x1, blocking collectives, local(): lax.all_gather(lse[:, :, 0].T, 'ctx', axis=0, tiled=True)  27 us
    all_gather x1, blocking collectives, local(): lax.all_gather(delta_rows, 'ctx', axis=0, tiled=True)  26.3 us
  transfers between devices with their start and end apart: 3, of which 2 were waited for; matrix products, arithmetic and copies ran while one was open for 6% of the time, Pallas kernels for 0%

commit v1 on v0

v1 whole, which is shorter than its diff:
```python
import math

import jax
import jax.numpy as jnp
from jax import lax
from jax.experimental import pallas as pl
from jax.experimental.pallas import tpu as pltpu
from jax.sharding import PartitionSpec as P

HD = 128
LOC = 256
BLK = 64
NEG = -1e30
MESH = pl.DeviceIdType.MESH
F32 = jnp.float32
BF16 = jnp.bfloat16
SCALE = HD**-0.5
C2 = SCALE * math.log2(math.e)


def nn(a, b):
    return lax.dot_general(a, b, (((1,), (0,)), ((), ())), preferred_element_type=F32)


def nt(a, b):
    return lax.dot_general(a, b, (((1,), (1,)), ((), ())), preferred_element_type=F32)


def softmax_t(scores, mask):
    s = jnp.where(mask, scores * C2, NEG)
    top = jnp.max(s, axis=0, keepdims=True)
    p = jnp.exp2(s - top)
    return p * (1.0 / jnp.sum(p, axis=0, keepdims=True))


def kernel(
    q_ref, k_ref, v_ref, og_ref, w_ref, sdoc_ref, ldoc_ref, place_ref,
    dq_ref, dk_ref, dv_ref, wg_ref,
    og_full, w_full, w_tr, stage, gstage, hot_in, hot_g, hot_p, hot_at, hot_attn, hot_grads, hot_acc,
    attn_in, grads_in, attn_all, attn_t, p_short, g_all, part, half_out, half_in,
    down_out, down_in, up_out, up_in, red, last_out, last_in,
    og_s, og_r, w_s, w_r, st_s, gs_s, hin_r, hg_r, ha_s, at_r, ho_s, gr_r,
    half_s, half_r, dn_s, dn_r, up_s, up_r, last_s, last_r,
):
    z = lax.axis_index("ctx")
    dp = lax.axis_index("dp")
    tp = lax.axis_index("tp")
    nz = 16
    y_hi, core = dp // 2, dp % 2
    y_lo, x = tp // 4, tp % 4
    row, other = y_lo * 4, (1 - y_lo) * 4
    xr, xl, xo = (x + 1) % 4, (x + 3) % 4, (x + 2) % 4
    dpo = (1 - y_hi) * 2 + core
    sib = y_hi * 2 + 1 - core
    right, left = {"tp": row + xr}, {"tp": row + xl}
    pair = {"tp": other + x}
    cross = {"dp": dpo, "tp": other + x}
    opposite = {"dp": dpo}
    sibling = {"dp": sib}
    zup, zdn = {"ctx": (z + 1) % nz}, {"ctx": (z + nz - 1) % nz}
    rel = (z + nz - 3 * core) % nz
    is_hot = (rel % 5 == 0) & (rel < 15)
    hot_h = rel // 5

    def rc(src, dst, ss, rs, dev):
        return pltpu.make_async_remote_copy(
            src_ref=src, dst_ref=dst, send_sem=ss, recv_sem=rs, device_id=dev, device_id_type=MESH
        )

    bar = pltpu.get_barrier_semaphore()
    for dev in (right, left, pair, cross, opposite, sibling):
        pl.semaphore_signal(bar, inc=1, device_id=dev, device_id_type=MESH)

    def greet(i, carry):
        pl.semaphore_signal(bar, inc=1, device_id={"ctx": (z + i) % nz}, device_id_type=MESH)
        return carry

    lax.fori_loop(1, nz, greet, 0)

    for h in range(3):
        hs = slice(h * HD, (h + 1) * HD)
        stage[h, 0] = q_ref[LOC:, hs]
        stage[h, 1] = k_ref[LOC:, hs]
        stage[h, 2] = v_ref[LOC:, hs]
    og_full[tp] = og_ref[...]
    w_full[dp] = w_ref[...]
    pl.semaphore_wait(bar, 21)

    lo, hi = pl.ds(0, 160), pl.ds(160, 160)
    wlo, whi = pl.ds(0, 320), pl.ds(320, 320)
    og = [
        (og_ref, og_full.at[tp], right, og_full.at[row + xl]),
        (og_ref, og_full.at[tp], left, og_full.at[row + xr]),
        (og_ref, og_full.at[tp], pair, og_full.at[other + x]),
        (og_full.at[row + xl, lo], og_full.at[row + xl, lo], right, og_full.at[row + xo, lo]),
        (og_full.at[row + xr, hi], og_full.at[row + xr, hi], left, og_full.at[row + xo, hi]),
        (og_full.at[other + x], og_full.at[other + x], right, og_full.at[other + xl]),
        (og_full.at[other + x], og_full.at[other + x], left, og_full.at[other + xr]),
        (og_full.at[other + xl, lo], og_full.at[other + xl, lo], right, og_full.at[other + xo, lo]),
        (og_full.at[other + xr, hi], og_full.at[other + xr, hi], left, og_full.at[other + xo, hi]),
    ]
    wg = [
        (w_ref.at[wlo], w_tr.at[0], pair, w_tr.at[0]),
        (w_ref.at[whi], w_tr.at[1], cross, w_tr.at[1]),
        (w_ref, w_full.at[dp], sibling, w_full.at[sib]),
        (w_tr.at[0], w_full.at[dp, wlo], cross, w_full.at[dpo, wlo]),
        (w_tr.at[1], w_full.at[dpo, whi], pair, w_full.at[dpo, whi]),
        (w_full.at[dpo, wlo], w_full.at[dpo, wlo], sibling, w_full.at[(1 - y_hi) * 2 + 1 - core, wlo]),
        (w_full.at[dpo, whi], w_full.at[dpo, whi], sibling, w_full.at[(1 - y_hi) * 2 + 1 - core, whi]),
    ]

    def og_go(i):
        src, dst, dev, _ = og[i]
        rc(src, dst, og_s.at[i], og_r.at[i], dev).start()

    def og_wait(i):
        land = og[i][3]
        rc(land, land, og_s.at[i], og_r.at[i], og[i][2]).wait_recv()

    def w_go(i):
        src, dst, dev, _ = wg[i]
        rc(src, dst, w_s.at[i], w_r.at[i], dev).start()

    def w_wait(i):
        land = wg[i][3]
        rc(land, land, w_s.at[i], w_r.at[i], wg[i][2]).wait_recv()

    for i in (2, 0, 1):
        og_go(i)
    for i in (0, 1, 2):
        w_go(i)

    def owner(h):
        return 5 * h + 3 * core

    def to_hot(h):
        return rc(stage.at[h], hot_in.at[z], st_s.at[h], hin_r.at[z], {"ctx": owner(h)})

    def g_to_hot(h):
        return rc(gstage.at[h], hot_g.at[z], gs_s.at[h], hg_r.at[z], {"ctx": owner(h)})

    for h in range(3):
        @pl.when(z != owner(h))
        def _():
            to_hot(h).start()

        @pl.when(z == owner(h))
        def _():
            hot_in[z] = stage[h]

    sid = sdoc_ref[...].astype(F32)
    sid_col = jnp.broadcast_to(sid, (HD, LOC)).T
    sid_col = jnp.concatenate([sid_col, sid_col], axis=1)
    kk = lax.broadcasted_iota(jnp.int32, (LOC, LOC), 0)
    qq = lax.broadcasted_iota(jnp.int32, (LOC, LOC), 1)
    smask = (kk <= qq) & (sid_col == sid)
    for h in range(3):
        hs = slice(h * HD, (h + 1) * HD)
        p = softmax_t(nt(k_ref[:LOC, hs], q_ref[:LOC, hs]), smask).astype(BF16)
        p_short[h] = p
        at = nn(v_ref[:LOC, hs].T, p).astype(BF16).astype(F32)
        attn_t[h] = at
        attn_all[:LOC, hs] = at.T.astype(BF16)

    og_wait(2)
    og_go(5)
    og_go(6)
    og_wait(0)
    og_go(3)
    og_wait(1)
    og_go(4)
    w_wait(0)
    w_go(3)
    w_wait(1)
    w_go(4)
    og_wait(5)
    og_go(7)
    og_wait(6)
    og_go(8)

    def each_other(fn):
        def body(i, carry):
            fn((z + i) % nz)
            return carry

        lax.fori_loop(1, nz, body, 0)

    def attn_back(c):
        return rc(hot_attn.at[c], attn_in.at[hot_h], ha_s.at[c], at_r.at[hot_h], {"ctx": c})

    def grads_back(c):
        return rc(hot_grads.at[c], grads_in.at[hot_h], ho_s.at[c], gr_r.at[hot_h], {"ctx": c})

    @pl.when(is_hot)
    def _():
        each_other(lambda c: rc(hot_in.at[c], hot_in.at[c], st_s.at[0], hin_r.at[c], zup).wait_recv())
        lane = lax.broadcasted_iota(jnp.int32, (1, 1024), 1)
        blk = lane // BLK
        place = jnp.zeros((1, 1024), jnp.int32)
        for c in range(nz):
            place = jnp.where(blk == c, place_ref[0, c], place)
        qpos = place * BLK + lane % BLK
        total = jnp.sum(ldoc_ref[...].astype(F32), axis=1, keepdims=True)
        cut = 1024 - total.astype(jnp.int32)
        qlo = jnp.where(qpos >= cut, cut, 0)
        k_all = hot_in[:, 1].reshape(1024, HD)
        v_t = hot_in[:, 2].reshape(1024, HD).T
        for t in range(4):
            ts = slice(t * 256, (t + 1) * 256)
            q_t = hot_in[4 * t : 4 * t + 4, 0].reshape(256, HD)
            s = nt(k_all, q_t)
            spot = lax.broadcasted_iota(jnp.int32, (BLK, 256), 0)
            kpos = jnp.concatenate([spot + place_ref[0, c] * BLK for c in range(nz)], axis=0)
            mask = (kpos <= qpos[:, ts]) & (kpos >= qlo[:, ts])
            p = softmax_t(s, mask).astype(BF16)
            hot_p[:, ts] = p
            at = nn(v_t, p).astype(BF16).astype(F32)
            hot_at[:, ts] = at
            hot_attn[4 * t : 4 * t + 4] = at.T.astype(BF16).reshape(4, BLK, HD)
        each_other(lambda c: attn_back(c).start())

    w_wait(3)
    w_go(5)
    w_wait(4)
    w_go(6)
    w_wait(2)
    og_wait(3)
    og_wait(4)
    og_wait(7)
    og_wait(8)
    w_wait(5)
    w_wait(6)

    acc = jnp.zeros((320, 384), F32)
    for t in range(8):
        acc += nn(og_full[t], w_full[t // 2, (t % 2) * 320 : (t % 2) * 320 + 320])
    g_all[...] = acc.astype(BF16)
    for h in range(3):
        gstage[h] = g_all[LOC:, h * HD : (h + 1) * HD]
    for h in range(3):
        @pl.when(z != owner(h))
        def _():
            g_to_hot(h).start()

        @pl.when(z == owner(h))
        def _():
            hot_g[z] = gstage[h]

    for h in range(3):
        hs = slice(h * HD, (h + 1) * HD)

        @pl.when(z != owner(h))
        def _():
            rc(attn_in.at[h], attn_in.at[h], gs_s.at[h], at_r.at[h], zup).wait_recv()
            attn_all[LOC:, hs] = attn_in[h]

        @pl.when(z == owner(h))
        def _():
            attn_all[LOC:, hs] = hot_attn[z]

    for t in range(8):
        w = nn(og_full[t].T, attn_all[...])
        for g in range(8):
            c, d = t * 2 + g // 4, g % 4
            part[d % 2, c, (d // 2) * 40 : (d // 2) * 40 + 40] = w[g * 40 : g * 40 + 40]
    half_out[...] = part[1 - core].astype(BF16)
    half = rc(half_out, half_in, half_s, half_r, sibling)
    half.start()

    for h in range(3):
        hs = slice(h * HD, (h + 1) * HD)
        g = g_all[:LOC, hs]
        v, k = v_ref[:LOC, hs], k_ref[:LOC, hs]
        delta = jnp.sum(g.T.astype(F32) * attn_t[h], axis=0, keepdims=True)
        p = p_short[h]
        ds = (p.astype(F32) * (nt(v, g) - delta)).astype(BF16)
        dk_ref[:LOC, hs] = (nn(ds, q_ref[:LOC, hs]) * SCALE).astype(BF16)
        dv_ref[:LOC, hs] = nn(p, g).astype(BF16)
        dq_ref[:LOC, hs] = (nn(k.T, ds).T * SCALE).astype(BF16)

    half.wait_recv()
    red[...] = part[core] + half_in[...].astype(F32)

    def hot_back(t):
        ts = slice(t * 256, (t + 1) * 256)
        if t == 0:
            each_other(lambda c: rc(hot_g.at[c], hot_g.at[c], gs_s.at[0], hg_r.at[c], zup).wait_recv())
        g = hot_g[4 * t : 4 * t + 4].reshape(256, HD)
        q = hot_in[4 * t : 4 * t + 4, 0].reshape(256, HD)
        delta = jnp.sum(g.T.astype(F32) * hot_at[:, ts], axis=0, keepdims=True)
        p = hot_p[:, ts]
        ds = (p.astype(F32) * (nt(hot_in[:, 2].reshape(1024, HD), g) - delta)).astype(BF16)
        dk = nn(ds, q)
        dv = nn(p, g)
        if t == 0:
            hot_acc[0] = dk
            hot_acc[1] = dv
        else:
            hot_acc[0] += dk
            hot_acc[1] += dv
        dq = nn(hot_in[:, 1].reshape(1024, HD).T, ds).T * SCALE
        hot_grads[4 * t : 4 * t + 4, 0] = dq.astype(BF16).reshape(4, BLK, HD)
        if t == 3:
            hot_grads[:, 1] = (hot_acc[0] * SCALE).astype(BF16).reshape(nz, BLK, HD)
            hot_grads[:, 2] = hot_acc[1].astype(BF16).reshape(nz, BLK, HD)
            each_other(lambda c: grads_back(c).start())

    def down(s):
        return rc(down_out.at[s], down_in.at[s], dn_s.at[s], dn_r.at[s], zdn)

    def up(s):
        return rc(up_out.at[s], up_in.at[s], up_s.at[s], up_r.at[s], zup)

    for s in range(8):
        v = red[(z + 8 + s) % nz]
        if s > 0:
            down(s - 1).wait_recv()
            v = v + down_in[s - 1].astype(F32)
        down_out[s] = v.astype(BF16)
        down(s).start()
        if s < 7:
            v = red[(z + 7 - s) % nz]
            if s > 0:
                up(s - 1).wait_recv()
                v = v + up_in[s - 1].astype(F32)
            up_out[s] = v.astype(BF16)
            up(s).start()
        if 1 <= s <= 4:
            pl.when(is_hot)(lambda: hot_back(s - 1))
    up(6).wait_recv()
    down(7).wait_recv()
    red[z] = red[z] + up_in[6].astype(F32) + down_in[7].astype(F32)
    last_out[0] = red[z, :40]
    last_out[1] = red[z, 40:]
    last = rc(last_out.at[1 - y_hi], last_in, last_s, last_r, opposite)
    last.start()

    for h in range(3):
        hs = slice(h * HD, (h + 1) * HD)

        @pl.when(z != owner(h))
        def _():
            rc(grads_in.at[h], grads_in.at[h], gs_s.at[h], gr_r.at[h], zup).wait_recv()
            dq_ref[LOC:, hs] = grads_in[h, 0]
            dk_ref[LOC:, hs] = grads_in[h, 1]
            dv_ref[LOC:, hs] = grads_in[h, 2]

        @pl.when(z == owner(h))
        def _():
            dq_ref[LOC:, hs] = hot_grads[z, 0]
            dk_ref[LOC:, hs] = hot_grads[z, 1]
            dv_ref[LOC:, hs] = hot_grads[z, 2]

    last.wait_recv()
    wg_ref[...] = last_out[y_hi] + last_in[...]

    for i in range(9):
        rc(og[i][0], og[i][1], og_s.at[i], og_r.at[i], og[i][2]).wait_send()
    for i in range(7):
        rc(wg[i][0], wg[i][1], w_s.at[i], w_r.at[i], wg[i][2]).wait_send()
    for h in range(3):
        @pl.when(z != owner(h))
        def _():
            to_hot(h).wait_send()
            g_to_hot(h).wait_send()

    @pl.when(is_hot)
    def _():
        each_other(lambda c: attn_back(c).wait_send())
        each_other(lambda c: grads_back(c).wait_send())

    half.wait_send()
    for s in range(8):
        down(s).wait_send()
        if s < 7:
            up(s).wait_send()
    last.wait_send()


def local(queries, keys, values, out_grad, out_weight, short_docs, long_docs, block_place):
    vm = pl.BlockSpec(memory_space=pltpu.VMEM)
    dma = pltpu.SemaphoreType.DMA
    dq, dk, dv, wg = pl.pallas_call(
        kernel,
        out_shape=(
            jax.ShapeDtypeStruct((320, 384), BF16),
            jax.ShapeDtypeStruct((320, 384), BF16),
            jax.ShapeDtypeStruct((320, 384), BF16),
            jax.ShapeDtypeStruct((40, 384), F32),
        ),
        in_specs=[vm] * 7 + [pl.BlockSpec(memory_space=pltpu.SMEM)],
        out_specs=(vm,) * 4,
        scratch_shapes=[
            pltpu.VMEM((8, 320, 320), BF16),
            pltpu.VMEM((4, 640, 384), BF16),
            pltpu.VMEM((2, 320, 384), BF16),
            pltpu.VMEM((3, 3, 64, 128), BF16),
            pltpu.VMEM((3, 64, 128), BF16),
            pltpu.VMEM((16, 3, 64, 128), BF16),
            pltpu.VMEM((16, 64, 128), BF16),
            pltpu.VMEM((1024, 1024), BF16),
            pltpu.VMEM((128, 1024), F32),
            pltpu.VMEM((16, 64, 128), BF16),
            pltpu.VMEM((16, 3, 64, 128), BF16),
            pltpu.VMEM((2, 1024, 128), F32),
            pltpu.VMEM((3, 64, 128), BF16),
            pltpu.VMEM((3, 3, 64, 128), BF16),
            pltpu.VMEM((320, 384), BF16),
            pltpu.VMEM((3, 128, 256), F32),
            pltpu.VMEM((3, 256, 256), BF16),
            pltpu.VMEM((320, 384), BF16),
            pltpu.VMEM((2, 16, 80, 384), F32),
            pltpu.VMEM((16, 80, 384), BF16),
            pltpu.VMEM((16, 80, 384), BF16),
            pltpu.VMEM((8, 80, 384), BF16),
            pltpu.VMEM((8, 80, 384), BF16),
            pltpu.VMEM((7, 80, 384), BF16),
            pltpu.VMEM((7, 80, 384), BF16),
            pltpu.VMEM((16, 80, 384), F32),
            pltpu.VMEM((2, 40, 384), F32),
            pltpu.VMEM((40, 384), F32),
            dma((9,)), dma((9,)), dma((7,)), dma((7,)),
            dma((3,)), dma((3,)), dma((16,)), dma((16,)),
            dma((16,)), dma((3,)), dma((16,)), dma((3,)),
            dma, dma, dma((8,)), dma((8,)), dma((7,)), dma((7,)), dma, dma,
        ],
        compiler_params=pltpu.CompilerParams(
            collective_id=0, has_side_effects=True, vmem_limit_bytes=50 * 1024 * 1024
        ),
        name="attention_grads",
    )(
        queries[0, 0], keys[0, 0], values[0, 0], out_grad[0, 0], out_weight,
        short_docs[0], long_docs, block_place,
    )
    shape = queries.shape
    return dq.reshape(shape), dk.reshape(shape), dv.reshape(shape), wg


def solution(mesh):
    placed = (
        P("dp", "ctx", None, "tp"),
        P("dp", "ctx", None, "tp"),
        P("dp", "ctx", None, "tp"),
        P("dp", "ctx", None, "tp"),
        P("dp", "tp"),
        P("dp", "ctx", None),
        P("dp", None),
        P("dp", None),
    )
    return jax.shard_map(
        local,
        mesh=mesh,
        in_specs=placed,
        out_specs=(
            P("dp", "ctx", None, "tp"),
            P("dp", "ctx", None, "tp"),
            P("dp", "ctx", None, "tp"),
            P(("ctx", "dp"), "tp"),
        ),
        check_vma=False,
    )
```

time: 668 us -> 96.3 us (0.14)
  waiting for transfers between devices: 393 us -> 0 us
  blocking collectives: 195 us -> 0 us
  Pallas kernels: 0 us -> 86.2 us
  local copies, waits for them, and re-layouts: 33.3 us -> 8.18 us
  matrix products: 21.9 us -> 0 us
  between operations: 15.6 us -> 0.67 us
  other arithmetic: 8.02 us -> 0 us
    unnamed x4 -> x0, waiting for transfers between devices: 390 us -> none
    all_gather x6 -> x0, blocking collectives: 195 us -> none  [the longest x1 40.2 us: local(): lax.all_gather(k_long, 'ctx', axis=0, tiled=True)]
    pallas_call x0 -> x1, Pallas kernels: none -> 86.2 us  [local(): pl.pallas_call(kernel, out_shape=(jax.ShapeDtypeStruct((320, 384), BF16),...]
    dot_general x14 -> x0, matrix products: 21.9 us -> none  [the longest x1 4.46 us: local(): lax.dot_general(cols, attn_all, (((0,), (0,)), ((), ())), preferred_eleme...]
    all_gather x7 -> x0, local copies, waits for them, and re-layouts: 11.8 us -> none  [the longest x1 8.57 us: local(): grads_full = lax.all_gather(out_grad[0, 0], 'tp', axis=1, tiled=True)]
  transfers between devices with their start and end apart: 3 -> 0, of which waited for: 2 -> 0; matrix products, arithmetic and copies ran while one was open for 6% -> 0% of each run, Pallas kernels for 0% -> 0%
where the time goes in v1:
time: 96.3 us; the launch traced here: 95 us
  Pallas kernels  86.2 us (90%)
  local copies, waits for them, and re-layouts  8.18 us (8%)
    pallas_call x1, Pallas kernels, local(): pl.pallas_call(kernel, out_shape=(jax.ShapeDtypeStruct((320, 384), BF16),...  86.2 us
    unnamed x20, local copies, waits for them, and re-layouts  8.18 us

profile of v1, /device:TPU:6, one launch (start us, length us, event | category | flops | bytes accessed | tf_op | source)
XLA Modules:
  0.0 95.0 jit_solution(5886362428219763316)
XLA Ops:
  0.6 0.0 copy-start.5
  0.6 0.0 copy-start.6
  0.7 0.0 copy-start.7
  0.7 0.7 copy-done.5
  1.3 0.0 copy-done.6
  1.3 0.0 copy-done.7
  1.3 0.0 copy-start
  1.3 1.0 %copy-done = bf16[640,384]{1,0:T(8,128)(2,1)S(1)} copy-done((bf16[640,384]{1,0:T(8,128)(2,1)S(1)}, bf16[640,384]{1,0:T(8,128)(2,1)}, u32[]{:S(2)}) %copy-start) | copy-done | bytes 491544
  2.4 0.0 copy-start.1
  2.4 0.9 copy-done.1
  3.3 0.0 copy-start.2
  3.3 0.9 copy-done.2
  4.3 0.0 copy-start.3
  4.3 0.9 copy-done.3
  5.2 0.0 copy-start.4
  5.2 0.9 copy-done.4
  6.1 86.2 %attention_grads.1 = (bf16[320,384]{1,0:T(8,128)(2,1)S(1)}, bf16[320,384]{1,0:T(8,128)(2,1)S(1)}, bf16[320,384]{1,0:T(8,128)(2,1)S(1)}, f32[40,384]{1,0:T(8,128)S(1)}) custom-call(bf16[320,384]{1,0:T(8,128)(2,1)S(1)} %bitcast.8, bf16[320,384]{1,0:T(8,128)(2,1)S(1)} %bitcast.9, bf16[320,384]{1,0:T(8,128)(2,1)S(1)} %bitcast.10, bf16[320,320]{1,0:T(8,128)(2,1)S(1)} %bitcast.11, ...), custom_call_target="tpu_custom_call" | custom-call | tf_op jit(solution)/shard_map/attention_grads/pallas_call | solution.py:383
  92.3 0.7 copy.16
  93.0 0.7 copy.17
  93.7 0.7 copy.18
  94.4 0.6 copy.19
Async XLA Ops:
  0.6 0.7 copy-start.5
  0.6 0.7 copy-start.6
  0.7 0.7 copy-start.7
  1.3 1.0 %copy-start = (bf16[640,384]{1,0:T(8,128)(2,1)S(1)}, bf16[640,384]{1,0:T(8,128)(2,1)}, u32[]{:S(2)}) copy-start(bf16[640,384]{1,0:T(8,128)(2,1)} %w_ref.1) | copy-start | bytes 1474564
  2.4 0.9 copy-start.1
  3.3 0.9 copy-start.2
  4.3 0.9 copy-start.3
  5.2 0.9 copy-start.4

commit v2 on v1

v2 whole, which is shorter than its diff:
```python
import math

import jax
import jax.numpy as jnp
from jax import lax
from jax.experimental import pallas as pl
from jax.experimental.pallas import tpu as pltpu
from jax.sharding import PartitionSpec as P

HD = 128
LOC = 256
BLK = 64
NEG = -1e30
MESH = pl.DeviceIdType.MESH
F32 = jnp.float32
BF16 = jnp.bfloat16
SCALE = HD**-0.5
C2 = SCALE * math.log2(math.e)


def nn(a, b):
    return lax.dot_general(a, b, (((1,), (0,)), ((), ())), preferred_element_type=F32)


def nt(a, b):
    return lax.dot_general(a, b, (((1,), (1,)), ((), ())), preferred_element_type=F32)


def softmax_t(scores, mask):
    s = jnp.where(mask, scores * C2, NEG)
    top = jnp.max(s, axis=0, keepdims=True)
    p = jnp.exp2(s - top)
    return p * (1.0 / jnp.sum(p, axis=0, keepdims=True))


def kernel(
    q_hbm, k_hbm, v_hbm, og_hbm, w_hbm, sdoc_hbm, ldoc_hbm, place_hbm,
    dq_ref, dk_ref, dv_ref, wg_ref,
    q_ref, k_ref, v_ref, sdoc_ref, ldoc_ref, place_ref,
    og_full, og_t, w_full, stage, gstage, hot_in, hot_g, hot_kt, hot_p, hot_at, hot_attn, hot_grads, hot_acc,
    attn_in, grads_in, attn_all, attn_t, p_short, g_acc, g_all, half_out, half_in,
    down_out, down_in, up_out, up_in, red, last_out, last_in,
    in_s, og_s, og_r, w_s, w_r, st_s, gs_s, hin_r, hg_r, ha_s, at_r, ho_s, gr_r,
    half_s, half_r, dn_s, dn_r, up_s, up_r, last_s, last_r,
):
    z = lax.axis_index("ctx")
    dp = lax.axis_index("dp")
    tp = lax.axis_index("tp")
    nz = 16
    y_hi, core = dp // 2, dp % 2
    y_lo, x = tp // 4, tp % 4
    row, other = y_lo * 4, (1 - y_lo) * 4
    xr, xl, xo = (x + 1) % 4, (x + 3) % 4, (x + 2) % 4
    dpo = (1 - y_hi) * 2 + core
    sib = y_hi * 2 + 1 - core
    sibo = (1 - y_hi) * 2 + 1 - core
    right, left = {"tp": row + xr}, {"tp": row + xl}
    pair = {"tp": other + x}
    opposite = {"dp": dpo}
    sibling = {"dp": sib}
    zup, zdn = {"ctx": (z + 1) % nz}, {"ctx": (z + nz - 1) % nz}
    rel = (z + nz - 3 * core) % nz
    is_hot = (rel % 5 == 0) & (rel < 15)
    hot_h = rel // 5

    def rc(src, dst, ss, rs, dev):
        return pltpu.make_async_remote_copy(
            src_ref=src, dst_ref=dst, send_sem=ss, recv_sem=rs, device_id=dev, device_id_type=MESH
        )

    loads = [
        pltpu.make_async_copy(src, dst, in_s.at[i])
        for i, (src, dst) in enumerate(
            (
                (og_hbm, og_full.at[tp]), (k_hbm, k_ref), (q_hbm, q_ref), (v_hbm, v_ref),
                (w_hbm, w_full.at[dp]), (sdoc_hbm, sdoc_ref), (ldoc_hbm, ldoc_ref), (place_hbm, place_ref),
            )
        )
    ]
    for load in loads:
        load.start()

    bar = pltpu.get_barrier_semaphore()
    for dev in (right, left, pair, opposite, sibling):
        pl.semaphore_signal(bar, inc=1, device_id=dev, device_id_type=MESH)

    def greet(i, carry):
        pl.semaphore_signal(bar, inc=1, device_id={"ctx": (z + i) % nz}, device_id_type=MESH)
        return carry

    lax.fori_loop(1, nz, greet, 0)
    for load in loads:
        load.wait()
    pl.semaphore_wait(bar, 20)

    lo, hi = pl.ds(0, 160), pl.ds(160, 160)
    og = [
        (tp, lo, right, row + xl),
        (tp, hi, right, row + xl),
        (other + x, lo, right, other + xl),
        (row + xl, lo, right, row + xo),
        (other + xl, lo, right, other + xo),
        (tp, hi, left, row + xr),
        (tp, lo, left, row + xr),
        (other + x, hi, left, other + xr),
        (row + xr, hi, left, row + xo),
        (other + xr, hi, left, other + xo),
        (tp, lo, pair, other + x),
        (tp, hi, pair, other + x),
        (other + x, hi, right, other + xl),
        (other + x, lo, left, other + xr),
    ]

    def og_copy(i):
        slot, rows, dev, _ = og[i]
        there = og_full.at[slot, rows]
        return rc(there, there, og_s.at[i], og_r.at[i], dev)

    def og_wait(i):
        _, rows, dev, slot = og[i]
        here = og_full.at[slot, rows]
        rc(here, here, og_s.at[i], og_r.at[i], dev).wait_recv()

    def turn(slot):
        t = og_full[slot].astype(F32).T.reshape(4, 2, 40, 320)
        og_t[slot, 0] = t[:, 0].reshape(160, 320).astype(BF16)
        og_t[slot, 1] = t[:, 1].reshape(160, 320).astype(BF16)

    def w_copy(i):
        slot, dev = ((dp, opposite), (dp, sibling), (dpo, sibling))[i]
        there = w_full.at[slot]
        return rc(there, there, w_s.at[i], w_r.at[i], dev)

    def w_wait(i):
        slot = (dpo, sib, sibo)[i]
        here = w_full.at[slot]
        rc(here, here, w_s.at[i], w_r.at[i], sibling).wait_recv()

    for i in (10, 0, 5, 11, 1, 6):
        og_copy(i).start()
    w_copy(0).start()

    def owner(h):
        return 5 * h + 3 * core

    def to_hot(h):
        return rc(stage.at[h], hot_in.at[z], st_s.at[h], hin_r.at[z], {"ctx": owner(h)})

    def g_to_hot(h):
        return rc(gstage.at[h], hot_g.at[z], gs_s.at[h], hg_r.at[z], {"ctx": owner(h)})

    for h in range(3):
        hs = slice(h * HD, (h + 1) * HD)
        stage[h, 0] = q_ref[LOC:, hs]
        stage[h, 1] = k_ref[LOC:, hs]
        stage[h, 2] = v_ref[LOC:, hs]
    for h in range(3):
        @pl.when(z != owner(h))
        def _():
            to_hot(h).start()

        @pl.when(z == owner(h))
        def _():
            hot_in[z] = stage[h]

    w_copy(1).start()

    sid = sdoc_ref[...].astype(F32)
    sid_col = jnp.broadcast_to(sid, (HD, LOC)).T
    sid_col = jnp.concatenate([sid_col, sid_col], axis=1)
    kk = lax.broadcasted_iota(jnp.int32, (LOC, LOC), 0)
    qq = lax.broadcasted_iota(jnp.int32, (LOC, LOC), 1)
    smask = (kk <= qq) & (sid_col == sid)

    def short_forward(h):
        hs = slice(h * HD, (h + 1) * HD)
        p = softmax_t(nt(k_ref[:LOC, hs], q_ref[:LOC, hs]), smask).astype(BF16)
        p_short[h] = p
        at = nn(v_ref[:LOC, hs].T, p).astype(BF16).astype(F32)
        attn_t[h] = at
        attn_all[:LOC, hs] = at.T.astype(BF16)

    short_forward(0)
    short_forward(1)
    og_wait(10)
    og_copy(2).start()
    og_wait(11)
    og_copy(7).start()
    og_wait(0)
    og_copy(3).start()
    og_wait(5)
    og_copy(8).start()
    og_copy(12).start()
    og_copy(13).start()
    og_wait(1)
    og_wait(6)
    short_forward(2)
    turn(tp)
    turn(other + x)
    og_wait(2)
    og_copy(4).start()
    og_wait(7)
    og_copy(9).start()

    def each_other(fn):
        def body(i, carry):
            fn((z + i) % nz)
            return carry

        lax.fori_loop(1, nz, body, 0)

    def attn_back(c):
        return rc(hot_attn.at[c], attn_in.at[hot_h], ha_s.at[c], at_r.at[hot_h], {"ctx": c})

    def grads_back(c):
        return rc(hot_grads.at[c], grads_in.at[hot_h], ho_s.at[c], gr_r.at[hot_h], {"ctx": c})

    @pl.when(is_hot)
    def _():
        each_other(lambda c: rc(hot_in.at[c], hot_in.at[c], st_s.at[0], hin_r.at[c], zup).wait_recv())
        lane = lax.broadcasted_iota(jnp.int32, (1, 1024), 1)
        blk = lane // BLK
        place = jnp.zeros((1, 1024), jnp.int32)
        for c in range(nz):
            place = jnp.where(blk == c, place_ref[0, c], place)
        qpos = place * BLK + lane % BLK
        total = jnp.sum(ldoc_ref[...].astype(F32), axis=1, keepdims=True)
        cut = 1024 - total.astype(jnp.int32)
        qlo = jnp.where(qpos >= cut, cut, 0)
        k_all = hot_in[:, 1].reshape(1024, HD)
        v_t = hot_in[:, 2].reshape(1024, HD).T
        for t in range(4):
            ts = slice(t * 256, (t + 1) * 256)
            q_t = hot_in[4 * t : 4 * t + 4, 0].reshape(256, HD)
            s = nt(k_all, q_t)
            spot = lax.broadcasted_iota(jnp.int32, (BLK, 256), 0)
            kpos = jnp.concatenate([spot + place_ref[0, c] * BLK for c in range(nz)], axis=0)
            mask = (kpos <= qpos[:, ts]) & (kpos >= qlo[:, ts])
            p = softmax_t(s, mask).astype(BF16)
            hot_p[:, ts] = p
            at = nn(v_t, p).astype(BF16).astype(F32)
            hot_at[:, ts] = at
            hot_attn[4 * t : 4 * t + 4] = at.T.astype(BF16).reshape(4, BLK, HD)
            for c in range(4 * t, 4 * t + 4):
                @pl.when(z != c)
                def _():
                    attn_back(c).start()
        hot_kt[...] = k_all.T

    turn(row + xl)
    turn(row + xr)
    og_wait(3)
    og_wait(8)
    turn(row + xo)
    og_wait(12)
    turn(other + xl)
    og_wait(13)
    turn(other + xr)
    og_wait(4)
    og_wait(9)
    turn(other + xo)

    def product(slot, k):
        return nn(og_full[2 * slot + k], w_full[slot, k * 320 : k * 320 + 320])

    w_wait(1)
    g_acc[...] = (product(dp, 0) + product(dp, 1)) + (product(sib, 0) + product(sib, 1))
    w_wait(0)
    w_copy(2).start()
    g_acc[...] += product(dpo, 0) + product(dpo, 1)
    w_wait(2)
    g_all[...] = (g_acc[...] + (product(sibo, 0) + product(sibo, 1))).astype(BF16)
    for h in range(3):
        gstage[h] = g_all[LOC:, h * HD : (h + 1) * HD]
    for h in range(3):
        @pl.when(z != owner(h))
        def _():
            g_to_hot(h).start()

        @pl.when(z == owner(h))
        def _():
            hot_g[z] = gstage[h]

    for h in range(3):
        hs = slice(h * HD, (h + 1) * HD)
        g = g_all[:LOC, hs]
        v, k = v_ref[:LOC, hs], k_ref[:LOC, hs]
        delta = jnp.sum(g.T.astype(F32) * attn_t[h], axis=0, keepdims=True)
        p = p_short[h]
        ds = (p.astype(F32) * (nt(v, g) - delta)).astype(BF16)
        dk_ref[:LOC, hs] = (nn(ds, q_ref[:LOC, hs]) * SCALE).astype(BF16)
        dv_ref[:LOC, hs] = nn(p, g).astype(BF16)
        dq_ref[:LOC, hs] = (nn(k.T, ds).T * SCALE).astype(BF16)

    for h in range(3):
        hs = slice(h * HD, (h + 1) * HD)

        @pl.when(z != owner(h))
        def _():
            rc(attn_in.at[h], attn_in.at[h], gs_s.at[h], at_r.at[h], zup).wait_recv()
            attn_all[LOC:, hs] = attn_in[h]

        @pl.when(z == owner(h))
        def _():
            attn_all[LOC:, hs] = hot_attn[z]

    sign = 1 - 2 * (z % 2)

    def nth(i):
        step = (i + 1) // 2
        return (z // 2 + 12 + (step if i % 2 == 0 else -step) * sign) % 8

    def half(i):
        there = pl.ds(2 * nth(i), 2)
        return rc(half_out.at[there], half_in.at[there], half_s.at[i], half_r.at[i], sibling)

    attn = attn_all[...]
    for i in range(8):
        t = nth(i)
        half_out[pl.ds(2 * t, 2)] = nn(og_t[t, 1 - core], attn).astype(BF16).reshape(2, 80, 384)
        half(i).start()
        red[pl.ds(2 * t, 2)] = nn(og_t[t, core], attn).reshape(2, 80, 384)

    subs = (pl.ds(0, 48), pl.ds(48, 32))

    def down(s, j):
        return rc(down_out.at[s, subs[j]], down_in.at[s, subs[j]], dn_s.at[s, j], dn_r.at[s, j], zdn)

    def up(s, j):
        return rc(up_out.at[s, subs[j]], up_in.at[s, subs[j]], up_s.at[s, j], up_r.at[s, j], zup)

    def mine(c, j):
        return red[c, subs[j]] + half_in[c, subs[j]].astype(F32)

    def ring(s):
        for i in {0: (0, 1), 1: (2, 3), 3: (4, 5), 5: (6, 7)}.get(s, ()):
            half(i).wait_recv()
        for j in range(2):
            v = mine((z + 8 + s) % nz, j)
            if s > 0:
                down(s - 1, j).wait_recv()
                v = v + down_in[s - 1, subs[j]].astype(F32)
            down_out[s, subs[j]] = v.astype(BF16)
            down(s, j).start()
            if s < 7:
                v = mine((z + 7 - s) % nz, j)
                if s > 0:
                    up(s - 1, j).wait_recv()
                    v = v + up_in[s - 1, subs[j]].astype(F32)
                up_out[s, subs[j]] = v.astype(BF16)
                up(s, j).start()

    def hot_back(t):
        ts = slice(t * 256, (t + 1) * 256)
        if t == 0:
            each_other(lambda c: rc(hot_g.at[c], hot_g.at[c], gs_s.at[0], hg_r.at[c], zup).wait_recv())
        g = hot_g[4 * t : 4 * t + 4].reshape(256, HD)
        q = hot_in[4 * t : 4 * t + 4, 0].reshape(256, HD)
        delta = jnp.sum(g.T.astype(F32) * hot_at[:, ts], axis=0, keepdims=True)
        p = hot_p[:, ts]
        ds = (p.astype(F32) * (nt(hot_in[:, 2].reshape(1024, HD), g) - delta)).astype(BF16)
        dk = nn(ds, q)
        dv = nn(p, g)
        if t > 0:
            dk += hot_acc[0]
            dv += hot_acc[1]
        dq = nn(hot_kt[...], ds).T * SCALE
        hot_grads[4 * t : 4 * t + 4, 0] = dq.astype(BF16).reshape(4, BLK, HD)
        if t < 3:
            hot_acc[0] = dk
            hot_acc[1] = dv
        else:
            hot_grads[:, 1] = (dk * SCALE).astype(BF16).reshape(nz, BLK, HD)
            hot_grads[:, 2] = dv.astype(BF16).reshape(nz, BLK, HD)
            each_other(lambda c: grads_back(c).start())

    for s in range(8):
        ring(s)
        if s < 4:
            pl.when(is_hot)(lambda: hot_back(s))
    for j in range(2):
        up(6, j).wait_recv()
        down(7, j).wait_recv()
    total = red[z] + half_in[z].astype(F32) + up_in[6].astype(F32) + down_in[7].astype(F32)
    last_out[...] = total.astype(BF16)
    red[z] = total
    theirs = pl.ds(pl.multiple_of(32 - 32 * y_hi, 16), 48)
    last = rc(last_out.at[theirs], last_in, last_s, last_r, opposite)
    last.start()

    for h in range(3):
        hs = slice(h * HD, (h + 1) * HD)

        @pl.when(z != owner(h))
        def _():
            rc(grads_in.at[h], grads_in.at[h], gs_s.at[h], gr_r.at[h], zup).wait_recv()
            dq_ref[LOC:, hs] = grads_in[h, 0]
            dk_ref[LOC:, hs] = grads_in[h, 1]
            dv_ref[LOC:, hs] = grads_in[h, 2]

        @pl.when(z == owner(h))
        def _():
            dq_ref[LOC:, hs] = hot_grads[z, 0]
            dk_ref[LOC:, hs] = hot_grads[z, 1]
            dv_ref[LOC:, hs] = hot_grads[z, 2]

    for i in range(14):
        og_copy(i).wait_send()
    for i in range(3):
        w_copy(i).wait_send()
    for h in range(3):
        @pl.when(z != owner(h))
        def _():
            to_hot(h).wait_send()
            g_to_hot(h).wait_send()

    @pl.when(is_hot)
    def _():
        each_other(lambda c: attn_back(c).wait_send())
        each_other(lambda c: grads_back(c).wait_send())

    for i in range(8):
        half(i).wait_send()
    for s in range(8):
        for j in range(2):
            down(s, j).wait_send()
            if s < 7:
                up(s, j).wait_send()
    last.wait()
    own = pl.ds(pl.multiple_of(40 * y_hi, 8), 40)
    came = last_in[...].astype(F32)
    wg_ref[...] = red[z, own] + jnp.where(y_hi == 0, came[:40], came[8:])


def local(queries, keys, values, out_grad, out_weight, short_docs, long_docs, block_place):
    vm = pl.BlockSpec(memory_space=pltpu.VMEM)
    hbm = pl.BlockSpec(memory_space=pltpu.HBM)
    dma = pltpu.SemaphoreType.DMA
    dq, dk, dv, wg = pl.pallas_call(
        kernel,
        out_shape=(
            jax.ShapeDtypeStruct((320, 384), BF16),
            jax.ShapeDtypeStruct((320, 384), BF16),
            jax.ShapeDtypeStruct((320, 384), BF16),
            jax.ShapeDtypeStruct((40, 384), F32),
        ),
        in_specs=[hbm] * 8,
        out_specs=(vm,) * 4,
        scratch_shapes=[
            pltpu.VMEM((320, 384), BF16),
            pltpu.VMEM((320, 384), BF16),
            pltpu.VMEM((320, 384), BF16),
            pltpu.VMEM((1, 256), jnp.int32),
            pltpu.VMEM((1, 1024), jnp.int32),
            pltpu.SMEM((1, 16), jnp.int32),
            pltpu.VMEM((8, 320, 320), BF16),
            pltpu.VMEM((8, 2, 160, 320), BF16),
            pltpu.VMEM((4, 640, 384), BF16),
            pltpu.VMEM((3, 3, 64, 128), BF16),
            pltpu.VMEM((3, 64, 128), BF16),
            pltpu.VMEM((16, 3, 64, 128), BF16),
            pltpu.VMEM((16, 64, 128), BF16),
            pltpu.VMEM((128, 1024), BF16),
            pltpu.VMEM((1024, 1024), BF16),
            pltpu.VMEM((128, 1024), F32),
            pltpu.VMEM((16, 64, 128), BF16),
            pltpu.VMEM((16, 3, 64, 128), BF16),
            pltpu.VMEM((2, 1024, 128), F32),
            pltpu.VMEM((3, 64, 128), BF16),
            pltpu.VMEM((3, 3, 64, 128), BF16),
            pltpu.VMEM((320, 384), BF16),
            pltpu.VMEM((3, 128, 256), F32),
            pltpu.VMEM((3, 256, 256), BF16),
            pltpu.VMEM((320, 384), F32),
            pltpu.VMEM((320, 384), BF16),
            pltpu.VMEM((16, 80, 384), BF16),
            pltpu.VMEM((16, 80, 384), BF16),
            pltpu.VMEM((8, 80, 384), BF16),
            pltpu.VMEM((8, 80, 384), BF16),
            pltpu.VMEM((7, 80, 384), BF16),
            pltpu.VMEM((7, 80, 384), BF16),
            pltpu.VMEM((16, 80, 384), F32),
            pltpu.VMEM((80, 384), BF16),
            pltpu.VMEM((48, 384), BF16),
            dma((8,)), dma((14,)), dma((14,)), dma((3,)), dma((3,)),
            dma((3,)), dma((3,)), dma((16,)), dma((16,)),
            dma((16,)), dma((3,)), dma((16,)), dma((3,)),
            dma((8,)), dma((8,)), dma((8, 2)), dma((8, 2)), dma((7, 2)), dma((7, 2)), dma, dma,
        ],
        compiler_params=pltpu.CompilerParams(
            collective_id=0, has_side_effects=True, vmem_limit_bytes=50 * 1024 * 1024
        ),
        name="attention_grads",
    )(
        *(
            pltpu.with_memory_space_constraint(a, pltpu.HBM)
            for a in (
                queries[0, 0], keys[0, 0], values[0, 0], out_grad[0, 0], out_weight,
                short_docs[0], long_docs, block_place,
            )
        )
    )
    shape = queries.shape
    return dq.reshape(shape), dk.reshape(shape), dv.reshape(shape), wg


def solution(mesh):
    placed = (
        P("dp", "ctx", None, "tp"),
        P("dp", "ctx", None, "tp"),
        P("dp", "ctx", None, "tp"),
        P("dp", "ctx", None, "tp"),
        P("dp", "tp"),
        P("dp", "ctx", None),
        P("dp", None),
        P("dp", None),
    )
    return jax.shard_map(
        local,
        mesh=mesh,
        in_specs=placed,
        out_specs=(
            P("dp", "ctx", None, "tp"),
            P("dp", "ctx", None, "tp"),
            P("dp", "ctx", None, "tp"),
            P(("ctx", "dp"), "tp"),
        ),
        check_vma=False,
    )
```

time: 96.3 us -> 83.6 us (0.87)
  Pallas kernels: 86.2 us -> 79.4 us
  local copies, waits for them, and re-layouts: 8.18 us -> 2.7 us
    pallas_call x1, Pallas kernels: 86.2 us -> 79.4 us  [local(): pl.pallas_call(kernel, out_shape=(jax.ShapeDtypeStruct((320, 384), BF16),...]
    unnamed x20 -> x4, local copies, waits for them, and re-layouts: 8.18 us -> 2.7 us
where the time goes in v2:
time: 83.6 us; the launch traced here: 82.8 us
  Pallas kernels  79.4 us (95%)
  local copies, waits for them, and re-layouts  2.7 us (3%)
    pallas_call x1, Pallas kernels, local(): pl.pallas_call(kernel, out_shape=(jax.ShapeDtypeStruct((320, 384), BF16),...  79.4 us
    unnamed x4, local copies, waits for them, and re-layouts  2.7 us

profile of v2, /device:TPU:6, one launch (start us, length us, event | category | flops | bytes accessed | tf_op | source)
XLA Modules:
  0.0 82.8 jit_solution(13455681022909889617)
XLA Ops:
  0.6 79.4 %attention_grads.1 = (bf16[320,384]{1,0:T(8,128)(2,1)S(1)}, bf16[320,384]{1,0:T(8,128)(2,1)S(1)}, bf16[320,384]{1,0:T(8,128)(2,1)S(1)}, f32[40,384]{1,0:T(8,128)S(1)}) custom-call(bf16[320,384]{1,0:T(8,128)(2,1)} %bitcast.11, bf16[320,384]{1,0:T(8,128)(2,1)} %bitcast.12, bf16[320,384]{1,0:T(8,128)(2,1)} %bitcast.13, bf16[320,320]{1,0:T(8,128)(2,1)} %bitcast.14, ...), custom_call_target="tpu_custom_call" | custom-call | tf_op jit(solution)/shard_map/attention_grads/pallas_call | solution.py:439
  80.0 0.7 copy.16
  80.7 0.7 copy.17
  81.4 0.7 copy.18
  82.1 0.6 copy.19

commit v3 on v2

--- a/solution.py
+++ b/solution.py
@@ -11,6 +11,7 @@
 LOC = 256
 BLK = 64
 NEG = -1e30
+OWNERS = ((0, 3), (5, 8), (10, 13))
 MESH = pl.DeviceIdType.MESH
 F32 = jnp.float32
 BF16 = jnp.bfloat16
@@ -39,9 +40,9 @@
     q_ref, k_ref, v_ref, sdoc_ref, ldoc_ref, place_ref,
     og_full, og_t, w_full, stage, gstage, hot_in, hot_g, hot_kt, hot_p, hot_at, hot_attn, hot_grads, hot_acc,
     attn_in, grads_in, attn_all, attn_t, p_short, g_acc, g_all, half_out, half_in,
-    down_out, down_in, up_out, up_in, red, last_out, last_in,
+    down_out, down_in, up_out, up_in, red, self_out, fin_in,
     in_s, og_s, og_r, w_s, w_r, st_s, gs_s, hin_r, hg_r, ha_s, at_r, ho_s, gr_r,
-    half_s, half_r, dn_s, dn_r, up_s, up_r, last_s, last_r,
+    half_s, half_r, dn_s, dn_r, up_s, up_r, fin_s, fin_r,
 ):
     z = lax.axis_index("ctx")
     dp = lax.axis_index("dp")
@@ -59,9 +60,10 @@
     opposite = {"dp": dpo}
     sibling = {"dp": sib}
     zup, zdn = {"ctx": (z + 1) % nz}, {"ctx": (z + nz - 1) % nz}
-    rel = (z + nz - 3 * core) % nz
-    is_hot = (rel % 5 == 0) & (rel < 15)
-    hot_h = rel // 5
+    zup_o, zdn_o = {"ctx": (z + 1) % nz, "dp": dpo}, {"ctx": (z + nz - 1) % nz, "dp": dpo}
+    owners = [jnp.where(core == 0, a, b) for a, b in OWNERS]
+    is_hot = (z == owners[0]) | (z == owners[1]) | (z == owners[2])
+    hot_h = jnp.where(z == owners[1], 1, jnp.where(z == owners[2], 2, 0))
 
     def rc(src, dst, ss, rs, dev):
         return pltpu.make_async_remote_copy(
@@ -81,17 +83,23 @@
         load.start()
 
     bar = pltpu.get_barrier_semaphore()
-    for dev in (right, left, pair, opposite, sibling):
+    for dev in (right, left, pair, opposite, sibling, zup_o, zdn_o):
         pl.semaphore_signal(bar, inc=1, device_id=dev, device_id_type=MESH)
 
     def greet(i, carry):
         pl.semaphore_signal(bar, inc=1, device_id={"ctx": (z + i) % nz}, device_id_type=MESH)
         return carry
 
-    lax.fori_loop(1, nz, greet, 0)
+    for dev in (zup, zdn):
+        pl.semaphore_signal(bar, inc=1, device_id=dev, device_id_type=MESH)
+
+    @pl.when(is_hot)
+    def _():
+        lax.fori_loop(1, nz, greet, 0)
+
     for load in loads:
         load.wait()
-    pl.semaphore_wait(bar, 20)
+    pl.semaphore_wait(bar, 12 - is_hot.astype(jnp.int32))
 
     lo, hi = pl.ds(0, 160), pl.ds(160, 160)
     og = [
@@ -126,25 +134,34 @@
         og_t[slot, 0] = t[:, 0].reshape(160, 320).astype(BF16)
         og_t[slot, 1] = t[:, 1].reshape(160, 320).astype(BF16)
 
+    wlo, whi, wall = pl.ds(0, 320), pl.ds(320, 320), pl.ds(0, 640)
+
     def w_copy(i):
-        slot, dev = ((dp, opposite), (dp, sibling), (dpo, sibling))[i]
-        there = w_full.at[slot]
+        slot, rows, dev = (
+            (dp, wlo, opposite), (dp, whi, opposite), (dp, wall, sibling), (dpo, wlo, sibling), (dpo, whi, sibling),
+        )[i]
+        there = w_full.at[slot, rows]
         return rc(there, there, w_s.at[i], w_r.at[i], dev)
 
     def w_wait(i):
-        slot = (dpo, sib, sibo)[i]
-        here = w_full.at[slot]
+        slot, rows = ((dpo, wlo), (dpo, whi), (sib, wall), (sibo, wlo), (sibo, whi))[i]
+        here = w_full.at[slot, rows]
         rc(here, here, w_s.at[i], w_r.at[i], sibling).wait_recv()
 
     for i in (10, 0, 5, 11, 1, 6):
         og_copy(i).start()
     w_copy(0).start()
+    w_copy(1).start()
 
     def owner(h):
-        return 5 * h + 3 * core
-
-    def to_hot(h):
-        return rc(stage.at[h], hot_in.at[z], st_s.at[h], hin_r.at[z], {"ctx": owner(h)})
+        return owners[h]
+
+    parts = (pl.ds(0, 2), pl.ds(2, 1))
+
+    def to_hot(h, n):
+        return rc(
+            stage.at[h, parts[n]], hot_in.at[z, parts[n]], st_s.at[h, n], hin_r.at[z, n], {"ctx": owner(h)}
+        )
 
     def g_to_hot(h):
         return rc(gstage.at[h], hot_g.at[z], gs_s.at[h], hg_r.at[z], {"ctx": owner(h)})
@@ -154,16 +171,18 @@
         stage[h, 0] = q_ref[LOC:, hs]
         stage[h, 1] = k_ref[LOC:, hs]
         stage[h, 2] = v_ref[LOC:, hs]
-    for h in range(3):
-        @pl.when(z != owner(h))
-        def _():
-            to_hot(h).start()
-
+    for n in range(2):
+        for h in range(3):
+            @pl.when(z != owner(h))
+            def _():
+                to_hot(h, n).start()
+
+    for h in range(3):
         @pl.when(z == owner(h))
         def _():
             hot_in[z] = stage[h]
 
-    w_copy(1).start()
+    w_copy(2).start()
 
     sid = sdoc_ref[...].astype(F32)
     sid_col = jnp.broadcast_to(sid, (HD, LOC)).T
@@ -212,12 +231,24 @@
     def attn_back(c):
         return rc(hot_attn.at[c], attn_in.at[hot_h], ha_s.at[c], at_r.at[hot_h], {"ctx": c})
 
-    def grads_back(c):
-        return rc(hot_grads.at[c], grads_in.at[hot_h], ho_s.at[c], gr_r.at[hot_h], {"ctx": c})
+    def dq_back(c):
+        part = pl.ds(0, 1)
+        return rc(hot_grads.at[c, part], grads_in.at[hot_h, part], ho_s.at[0, c], gr_r.at[0, hot_h], {"ctx": c})
+
+    def dkv_back(c):
+        part = pl.ds(1, 2)
+        return rc(hot_grads.at[c, part], grads_in.at[hot_h, part], ho_s.at[1, c], gr_r.at[1, hot_h], {"ctx": c})
 
     @pl.when(is_hot)
     def _():
-        each_other(lambda c: rc(hot_in.at[c], hot_in.at[c], st_s.at[0], hin_r.at[c], zup).wait_recv())
+        def hot_wait(n):
+            each_other(
+                lambda c: rc(
+                    hot_in.at[c, parts[n]], hot_in.at[c, parts[n]], st_s.at[0, n], hin_r.at[c, n], zup
+                ).wait_recv()
+            )
+
+        hot_wait(0)
         lane = lax.broadcasted_iota(jnp.int32, (1, 1024), 1)
         blk = lane // BLK
         place = jnp.zeros((1, 1024), jnp.int32)
@@ -228,17 +259,24 @@
         cut = 1024 - total.astype(jnp.int32)
         qlo = jnp.where(qpos >= cut, cut, 0)
         k_all = hot_in[:, 1].reshape(1024, HD)
+        spot = lax.broadcasted_iota(jnp.int32, (BLK, 256), 0)
+        kpos = jnp.concatenate([spot + place_ref[0, c] * BLK for c in range(nz)], axis=0)
+
+        def weigh(t):
+            ts = slice(t * 256, (t + 1) * 256)
+            q_t = hot_in[4 * t : 4 * t + 4, 0].reshape(256, HD)
+            mask = (kpos <= qpos[:, ts]) & (kpos >= qlo[:, ts])
+            hot_p[:, ts] = softmax_t(nt(k_all, q_t), mask).astype(BF16)
+
+        weigh(0)
+        weigh(1)
+        hot_wait(1)
         v_t = hot_in[:, 2].reshape(1024, HD).T
         for t in range(4):
             ts = slice(t * 256, (t + 1) * 256)
-            q_t = hot_in[4 * t : 4 * t + 4, 0].reshape(256, HD)
-            s = nt(k_all, q_t)
-            spot = lax.broadcasted_iota(jnp.int32, (BLK, 256), 0)
-            kpos = jnp.concatenate([spot + place_ref[0, c] * BLK for c in range(nz)], axis=0)
-            mask = (kpos <= qpos[:, ts]) & (kpos >= qlo[:, ts])
-            p = softmax_t(s, mask).astype(BF16)
-            hot_p[:, ts] = p
-            at = nn(v_t, p).astype(BF16).astype(F32)
+            if t > 1:
+                weigh(t)
+            at = nn(v_t, hot_p[:, ts]).astype(BF16).astype(F32)
             hot_at[:, ts] = at
             hot_attn[4 * t : 4 * t + 4] = at.T.astype(BF16).reshape(4, BLK, HD)
             for c in range(4 * t, 4 * t + 4):
@@ -263,12 +301,15 @@
     def product(slot, k):
         return nn(og_full[2 * slot + k], w_full[slot, k * 320 : k * 320 + 320])
 
-    w_wait(1)
+    w_wait(2)
     g_acc[...] = (product(dp, 0) + product(dp, 1)) + (product(sib, 0) + product(sib, 1))
     w_wait(0)
-    w_copy(2).start()
+    w_copy(3).start()
+    w_wait(1)
+    w_copy(4).start()
     g_acc[...] += product(dpo, 0) + product(dpo, 1)
-    w_wait(2)
+    w_wait(3)
+    w_wait(4)
     g_all[...] = (g_acc[...] + (product(sibo, 0) + product(sibo, 1))).astype(BF16)
     for h in range(3):
         gstage[h] = g_all[LOC:, h * HD : (h + 1) * HD]
@@ -341,14 +382,33 @@
                 down(s - 1, j).wait_recv()
                 v = v + down_in[s - 1, subs[j]].astype(F32)
             down_out[s, subs[j]] = v.astype(BF16)
-            down(s, j).start()
             if s < 7:
+                down(s, j).start()
                 v = mine((z + 7 - s) % nz, j)
                 if s > 0:
                     up(s - 1, j).wait_recv()
                     v = v + up_in[s - 1, subs[j]].astype(F32)
                 up_out[s, subs[j]] = v.astype(BF16)
-                up(s, j).start()
+                if s < 6:
+                    up(s, j).start()
+        if s == 5:
+            self_out[...] = (red[z] + half_in[z].astype(F32)).astype(BF16)
+            final(4).start()
+        if s == 6:
+            final(2).start()
+            final(3).start()
+        if s == 7:
+            final(0).start()
+            final(1).start()
+
+    ours, theirs = (pl.ds(pl.multiple_of(32 * k, 16), 48) for k in (y_hi, 1 - y_hi))
+
+    def final(i):
+        src, rows, dev = (
+            (down_out.at[7], ours, zdn), (down_out.at[7], theirs, zdn_o),
+            (up_out.at[6], ours, zup), (up_out.at[6], theirs, zup_o), (self_out, theirs, opposite),
+        )[i]
+        return rc(src.at[rows], fin_in.at[i], fin_s.at[i], fin_r.at[i], dev)
 
     def hot_back(t):
         ts = slice(t * 256, (t + 1) * 256)
@@ -366,34 +426,29 @@
             dv += hot_acc[1]
         dq = nn(hot_kt[...], ds).T * SCALE
         hot_grads[4 * t : 4 * t + 4, 0] = dq.astype(BF16).reshape(4, BLK, HD)
+        for c in range(4 * t, 4 * t + 4):
+            @pl.when(z != c)
+            def _():
+                dq_back(c).start()
         if t < 3:
             hot_acc[0] = dk
             hot_acc[1] = dv
         else:
             hot_grads[:, 1] = (dk * SCALE).astype(BF16).reshape(nz, BLK, HD)
             hot_grads[:, 2] = dv.astype(BF16).reshape(nz, BLK, HD)
-            each_other(lambda c: grads_back(c).start())
+            each_other(lambda c: dkv_back(c).start())
 
     for s in range(8):
         ring(s)
-        if s < 4:
-            pl.when(is_hot)(lambda: hot_back(s))
-    for j in range(2):
-        up(6, j).wait_recv()
-        down(7, j).wait_recv()
-    total = red[z] + half_in[z].astype(F32) + up_in[6].astype(F32) + down_in[7].astype(F32)
-    last_out[...] = total.astype(BF16)
-    red[z] = total
-    theirs = pl.ds(pl.multiple_of(32 - 32 * y_hi, 16), 48)
-    last = rc(last_out.at[theirs], last_in, last_s, last_r, opposite)
-    last.start()
-
+        if 2 <= s <= 5:
+            pl.when(is_hot)(lambda: hot_back(s - 2))
     for h in range(3):
         hs = slice(h * HD, (h + 1) * HD)
 
         @pl.when(z != owner(h))
         def _():
-            rc(grads_in.at[h], grads_in.at[h], gs_s.at[h], gr_r.at[h], zup).wait_recv()
+            for n, part in enumerate((pl.ds(0, 1), pl.ds(1, 2))):
+                rc(grads_in.at[h, part], grads_in.at[h, part], gs_s.at[h], gr_r.at[n, h], zup).wait_recv()
             dq_ref[LOC:, hs] = grads_in[h, 0]
             dk_ref[LOC:, hs] = grads_in[h, 1]
             dv_ref[LOC:, hs] = grads_in[h, 2]
@@ -406,30 +461,37 @@
 
     for i in range(14):
         og_copy(i).wait_send()
-    for i in range(3):
+    for i in range(5):
         w_copy(i).wait_send()
     for h in range(3):
         @pl.when(z != owner(h))
         def _():
-            to_hot(h).wait_send()
+            to_hot(h, 0).wait_send()
+            to_hot(h, 1).wait_send()
             g_to_hot(h).wait_send()
 
     @pl.when(is_hot)
     def _():
         each_other(lambda c: attn_back(c).wait_send())
-        each_other(lambda c: grads_back(c).wait_send())
+        each_other(lambda c: dq_back(c).wait_send())
+        each_other(lambda c: dkv_back(c).wait_send())
 
     for i in range(8):
         half(i).wait_send()
     for s in range(8):
         for j in range(2):
-            down(s, j).wait_send()
             if s < 7:
+                down(s, j).wait_send()
+            if s < 6:
                 up(s, j).wait_send()
-    last.wait()
-    own = pl.ds(pl.multiple_of(40 * y_hi, 8), 40)
-    came = last_in[...].astype(F32)
-    wg_ref[...] = red[z, own] + jnp.where(y_hi == 0, came[:40], came[8:])
+    for i in range(5):
+        final(i).wait()
+    total = red[z] + half_in[z].astype(F32)
+    low, high = total[:40], total[40:]
+    for i in range(5):
+        came = fin_in[i].astype(F32)
+        low, high = low + came[:40], high + came[8:]
+    wg_ref[...] = jnp.where(y_hi == 0, low, high)
 
 
 def local(queries, keys, values, out_grad, out_weight, short_docs, long_docs, block_place):
@@ -481,11 +543,11 @@
             pltpu.VMEM((7, 80, 384), BF16),
             pltpu.VMEM((16, 80, 384), F32),
             pltpu.VMEM((80, 384), BF16),
-            pltpu.VMEM((48, 384), BF16),
-            dma((8,)), dma((14,)), dma((14,)), dma((3,)), dma((3,)),
-            dma((3,)), dma((3,)), dma((16,)), dma((16,)),
-            dma((16,)), dma((3,)), dma((16,)), dma((3,)),
-            dma((8,)), dma((8,)), dma((8, 2)), dma((8, 2)), dma((7, 2)), dma((7, 2)), dma, dma,
+            pltpu.VMEM((5, 48, 384), BF16),
+            dma((8,)), dma((14,)), dma((14,)), dma((5,)), dma((5,)),
+            dma((3, 2)), dma((3,)), dma((16, 2)), dma((16,)),
+            dma((16,)), dma((3,)), dma((2, 16)), dma((2, 3)),
+            dma((8,)), dma((8,)), dma((8, 2)), dma((8, 2)), dma((7, 2)), dma((7, 2)), dma((5,)), dma((5,)),
         ],
         compiler_params=pltpu.CompilerParams(
             collective_id=0, has_side_effects=True, vmem_limit_bytes=50 * 1024 * 1024

time: 83.6 us -> 79.5 us (0.951)
  the two profiles are of different devices: /device:TPU:6 before, /device:TPU:2 now
where the time goes in v3:
time: 79.5 us; the launch traced here: 79.3 us
  Pallas kernels  76 us (96%)
  local copies, waits for them, and re-layouts  2.7 us (3%)
    pallas_call x1, Pallas kernels, local(): pl.pallas_call(kernel, out_shape=(jax.ShapeDtypeStruct((320, 384), BF16),...  76 us
    unnamed x4, local copies, waits for them, and re-layouts  2.7 us

profile of v3, /device:TPU:2, one launch (start us, length us, event | category | flops | bytes accessed | tf_op | source)
XLA Modules:
  0.0 79.3 jit_solution(16150349032006248194)
XLA Ops:
  0.6 76.0 %attention_grads.1 = (bf16[320,384]{1,0:T(8,128)(2,1)S(1)}, bf16[320,384]{1,0:T(8,128)(2,1)S(1)}, bf16[320,384]{1,0:T(8,128)(2,1)S(1)}, f32[40,384]{1,0:T(8,128)S(1)}) custom-call(bf16[320,384]{1,0:T(8,128)(2,1)} %bitcast.11, bf16[320,384]{1,0:T(8,128)(2,1)} %bitcast.12, bf16[320,384]{1,0:T(8,128)(2,1)} %bitcast.13, bf16[320,320]{1,0:T(8,128)(2,1)} %bitcast.14, ...), custom_call_target="tpu_custom_call" | custom-call | tf_op jit(solution)/shard_map/attention_grads/pallas_call | solution.py:501
  76.6 0.7 copy.16
  77.3 0.7 copy.17
  78.0 0.7 copy.18
  78.7 0.6 copy.19

commit v4 on v3

--- a/solution.py
+++ b/solution.py
@@ -11,7 +11,7 @@
 LOC = 256
 BLK = 64
 NEG = -1e30
-OWNERS = ((0, 3), (5, 8), (10, 13))
+OWNERS = ((0, 3), (6, 8), (11, 14))
 MESH = pl.DeviceIdType.MESH
 F32 = jnp.float32
 BF16 = jnp.bfloat16
@@ -324,17 +324,6 @@
 
     for h in range(3):
         hs = slice(h * HD, (h + 1) * HD)
-        g = g_all[:LOC, hs]
-        v, k = v_ref[:LOC, hs], k_ref[:LOC, hs]
-        delta = jnp.sum(g.T.astype(F32) * attn_t[h], axis=0, keepdims=True)
-        p = p_short[h]
-        ds = (p.astype(F32) * (nt(v, g) - delta)).astype(BF16)
-        dk_ref[:LOC, hs] = (nn(ds, q_ref[:LOC, hs]) * SCALE).astype(BF16)
-        dv_ref[:LOC, hs] = nn(p, g).astype(BF16)
-        dq_ref[:LOC, hs] = (nn(k.T, ds).T * SCALE).astype(BF16)
-
-    for h in range(3):
-        hs = slice(h * HD, (h + 1) * HD)
 
         @pl.when(z != owner(h))
         def _():
@@ -355,14 +344,17 @@
         there = pl.ds(2 * nth(i), 2)
         return rc(half_out.at[there], half_in.at[there], half_s.at[i], half_r.at[i], sibling)
 
-    attn = attn_all[...]
-    for i in range(8):
+    def piece(i):
         t = nth(i)
+        attn = attn_all[...]
         half_out[pl.ds(2 * t, 2)] = nn(og_t[t, 1 - core], attn).astype(BF16).reshape(2, 80, 384)
         half(i).start()
         red[pl.ds(2 * t, 2)] = nn(og_t[t, core], attn).reshape(2, 80, 384)
 
-    subs = (pl.ds(0, 48), pl.ds(48, 32))
+    for i in range(4):
+        piece(i)
+
+    subs = (pl.ds(0, 32), pl.ds(32, 32), pl.ds(64, 16))
 
     def down(s, j):
         return rc(down_out.at[s, subs[j]], down_in.at[s, subs[j]], dn_s.at[s, j], dn_r.at[s, j], zdn)
@@ -376,7 +368,7 @@
     def ring(s):
         for i in {0: (0, 1), 1: (2, 3), 3: (4, 5), 5: (6, 7)}.get(s, ()):
             half(i).wait_recv()
-        for j in range(2):
+        for j in range(3):
             v = mine((z + 8 + s) % nz, j)
             if s > 0:
                 down(s - 1, j).wait_recv()
@@ -438,7 +430,22 @@
             hot_grads[:, 2] = dv.astype(BF16).reshape(nz, BLK, HD)
             each_other(lambda c: dkv_back(c).start())
 
-    for s in range(8):
+    ring(0)
+    for i in range(4, 8):
+        piece(i)
+
+    for h in range(3):
+        hs = slice(h * HD, (h + 1) * HD)
+        g = g_all[:LOC, hs]
+        v, k = v_ref[:LOC, hs], k_ref[:LOC, hs]
+        delta = jnp.sum(g.T.astype(F32) * attn_t[h], axis=0, keepdims=True)
+        p = p_short[h]
+        ds = (p.astype(F32) * (nt(v, g) - delta)).astype(BF16)
+        dk_ref[:LOC, hs] = (nn(ds, q_ref[:LOC, hs]) * SCALE).astype(BF16)
+        dv_ref[:LOC, hs] = nn(p, g).astype(BF16)
+        dq_ref[:LOC, hs] = (nn(k.T, ds).T * SCALE).astype(BF16)
+
+    for s in range(1, 8):
         ring(s)
         if 2 <= s <= 5:
             pl.when(is_hot)(lambda: hot_back(s - 2))
@@ -479,7 +486,7 @@
     for i in range(8):
         half(i).wait_send()
     for s in range(8):
-        for j in range(2):
+        for j in range(3):
             if s < 7:
                 down(s, j).wait_send()
             if s < 6:
@@ -547,7 +554,7 @@
             dma((8,)), dma((14,)), dma((14,)), dma((5,)), dma((5,)),
             dma((3, 2)), dma((3,)), dma((16, 2)), dma((16,)),
             dma((16,)), dma((3,)), dma((2, 16)), dma((2, 3)),
-            dma((8,)), dma((8,)), dma((8, 2)), dma((8, 2)), dma((7, 2)), dma((7, 2)), dma((5,)), dma((5,)),
+            dma((8,)), dma((8,)), dma((8, 3)), dma((8, 3)), dma((7, 3)), dma((7, 3)), dma((5,)), dma((5,)),
         ],
         compiler_params=pltpu.CompilerParams(
             collective_id=0, has_side_effects=True, vmem_limit_bytes=50 * 1024 * 1024

time: 79.5 us -> 76.2 us (0.958)
  the two profiles are of different devices: /device:TPU:2 before, /device:TPU:6 now
where the time goes in v4:
time: 76.2 us; the launch traced here: 75.3 us
  Pallas kernels  71.9 us (94%)
  local copies, waits for them, and re-layouts  2.7 us (4%)
    pallas_call x1, Pallas kernels, local(): pl.pallas_call(kernel, out_shape=(jax.ShapeDtypeStruct((320, 384), BF16),...  71.9 us
    unnamed x4, local copies, waits for them, and re-layouts  2.7 us

profile of v4, /device:TPU:6, one launch (start us, length us, event | category | flops | bytes accessed | tf_op | source)
XLA Modules:
  0.0 75.3 jit_solution(15144678757915516977)
XLA Ops:
  0.6 71.9 %attention_grads.1 = (bf16[320,384]{1,0:T(8,128)(2,1)S(1)}, bf16[320,384]{1,0:T(8,128)(2,1)S(1)}, bf16[320,384]{1,0:T(8,128)(2,1)S(1)}, f32[40,384]{1,0:T(8,128)S(1)}) custom-call(bf16[320,384]{1,0:T(8,128)(2,1)} %bitcast.11, bf16[320,384]{1,0:T(8,128)(2,1)} %bitcast.12, bf16[320,384]{1,0:T(8,128)(2,1)} %bitcast.13, bf16[320,320]{1,0:T(8,128)(2,1)} %bitcast.14, ...), custom_call_target="tpu_custom_call" | custom-call | tf_op jit(solution)/shard_map/attention_grads/pallas_call | solution.py:508
  72.6 0.7 copy.16
  73.3 0.7 copy.17
  74.0 0.7 copy.18
  74.7 0.6 copy.19

commit v5 on v4

--- a/solution.py
+++ b/solution.py
@@ -39,7 +39,7 @@
     dq_ref, dk_ref, dv_ref, wg_ref,
     q_ref, k_ref, v_ref, sdoc_ref, ldoc_ref, place_ref,
     og_full, og_t, w_full, stage, gstage, hot_in, hot_g, hot_kt, hot_p, hot_at, hot_attn, hot_grads, hot_acc,
-    attn_in, grads_in, attn_all, attn_t, p_short, g_acc, g_all, half_out, half_in,
+    attn_in, grads_in, attn_all, attn_t, p_short, g_all, half_out, half_in,
     down_out, down_in, up_out, up_in, red, self_out, fin_in,
     in_s, og_s, og_r, w_s, w_r, st_s, gs_s, hin_r, hg_r, ha_s, at_r, ho_s, gr_r,
     half_s, half_r, dn_s, dn_r, up_s, up_r, fin_s, fin_r,
@@ -150,8 +150,6 @@
 
     for i in (10, 0, 5, 11, 1, 6):
         og_copy(i).start()
-    w_copy(0).start()
-    w_copy(1).start()
 
     def owner(h):
         return owners[h]
@@ -182,7 +180,8 @@
         def _():
             hot_in[z] = stage[h]
 
-    w_copy(2).start()
+    for i in range(3):
+        w_copy(i).start()
 
     sid = sdoc_ref[...].astype(F32)
     sid_col = jnp.broadcast_to(sid, (HD, LOC)).T
@@ -298,21 +297,26 @@
     og_wait(9)
     turn(other + xo)
 
-    def product(slot, k):
-        return nn(og_full[2 * slot + k], w_full[slot, k * 320 : k * 320 + 320])
+    def product(slot, k, rows):
+        return nn(og_full[2 * slot + k, rows], w_full[slot, k * 320 : k * 320 + 320])
+
+    def products(slot, rows):
+        return product(slot, 0, rows) + product(slot, 1, rows)
+
+    short_rows, long_rows = pl.ds(0, LOC), pl.ds(LOC, BLK)
 
     w_wait(2)
-    g_acc[...] = (product(dp, 0) + product(dp, 1)) + (product(sib, 0) + product(sib, 1))
+    grad = products(dp, long_rows) + products(sib, long_rows)
     w_wait(0)
     w_copy(3).start()
     w_wait(1)
     w_copy(4).start()
-    g_acc[...] += product(dpo, 0) + product(dpo, 1)
+    grad += products(dpo, long_rows)
     w_wait(3)
     w_wait(4)
-    g_all[...] = (g_acc[...] + (product(sibo, 0) + product(sibo, 1))).astype(BF16)
-    for h in range(3):
-        gstage[h] = g_all[LOC:, h * HD : (h + 1) * HD]
+    grad = (grad + products(sibo, long_rows)).astype(BF16)
+    for h in range(3):
+        gstage[h] = grad[:, h * HD : (h + 1) * HD]
     for h in range(3):
         @pl.when(z != owner(h))
         def _():
@@ -434,9 +438,13 @@
     for i in range(4, 8):
         piece(i)
 
+    g_all[...] = (
+        (products(dp, short_rows) + products(sib, short_rows)) + (products(dpo, short_rows) + products(sibo, short_rows))
+    ).astype(BF16)
+
     for h in range(3):
         hs = slice(h * HD, (h + 1) * HD)
-        g = g_all[:LOC, hs]
+        g = g_all[:, hs]
         v, k = v_ref[:LOC, hs], k_ref[:LOC, hs]
         delta = jnp.sum(g.T.astype(F32) * attn_t[h], axis=0, keepdims=True)
         p = p_short[h]
@@ -540,8 +548,7 @@
             pltpu.VMEM((320, 384), BF16),
             pltpu.VMEM((3, 128, 256), F32),
             pltpu.VMEM((3, 256, 256), BF16),
-            pltpu.VMEM((320, 384), F32),
-            pltpu.VMEM((320, 384), BF16),
+            pltpu.VMEM((256, 384), BF16),
             pltpu.VMEM((16, 80, 384), BF16),
             pltpu.VMEM((16, 80, 384), BF16),
             pltpu.VMEM((8, 80, 384), BF16),

time: 76.2 us -> 75.6 us (level)
  no operation moved by 1% of the time
where the time goes in v5:
time: 75.6 us; the launch traced here: 74.8 us
  Pallas kernels  71.4 us (94%)
  local copies, waits for them, and re-layouts  2.7 us (4%)
    pallas_call x1, Pallas kernels, local(): pl.pallas_call(kernel, out_shape=(jax.ShapeDtypeStruct((320, 384), BF16),...  71.4 us
    unnamed x4, local copies, waits for them, and re-layouts  2.7 us

profile of v5, /device:TPU:6, one launch (start us, length us, event | category | flops | bytes accessed | tf_op | source)
XLA Modules:
  0.0 74.8 jit_solution(3160405528874470136)
XLA Ops:
  0.6 71.4 %attention_grads.1 = (bf16[320,384]{1,0:T(8,128)(2,1)S(1)}, bf16[320,384]{1,0:T(8,128)(2,1)S(1)}, bf16[320,384]{1,0:T(8,128)(2,1)S(1)}, f32[40,384]{1,0:T(8,128)S(1)}) custom-call(bf16[320,384]{1,0:T(8,128)(2,1)} %bitcast.11, bf16[320,384]{1,0:T(8,128)(2,1)} %bitcast.12, bf16[320,384]{1,0:T(8,128)(2,1)} %bitcast.13, bf16[320,320]{1,0:T(8,128)(2,1)} %bitcast.14, ...), custom_call_target="tpu_custom_call" | custom-call | tf_op jit(solution)/shard_map/attention_grads/pallas_call | solution.py:516
  72.1 0.7 copy.16
  72.8 0.7 copy.17
  73.5 0.7 copy.18
  74.2 0.6 copy.19
